TPU v7x, 128 devices: a whole 4x4x4 slice. The times are simulated.
128 devices in a mesh: slide: 4 (over x_hi, core), seq: 32 (over z, x_lo, y).
Axes of the slice: x: 4 (x_hi: 2, x_lo: 2; x = x_hi * 2 + x_lo), y: 4, z: 4, core: 2. Of those that a mesh axis runs over, the one named last changes fastest.
Arguments:
- tile_count: int32 [4], P('slide'), may hold values from 4096 to 16384, as said below
- query_rows: bfloat16 [65536, 384], P(('slide', 'seq')), may hold values from -12 to 12
- key_rows: bfloat16 [65536, 384], P(('slide', 'seq')), may hold values from -12 to 12
- value_rows: bfloat16 [65536, 384], P(('slide', 'seq')), may hold values from -6 to 6
- out_grad: bfloat16 [65536, 768], P(('slide', 'seq')), may hold values from -6 to 6
- out_weight: bfloat16 [384, 768], replicated, may hold values from -0.3125 to 0.3125
Outputs:
- query_gradient: bfloat16 [65536, 384], P(('slide', 'seq'))
- key_gradient: bfloat16 [65536, 384], P(('slide', 'seq'))
- value_gradient: bfloat16 [65536, 384], P(('slide', 'seq'))
- weight_grad: float32 [384, 768], replicated
Inputs may be any that keep to these rules, and one draw needn't show every extreme that they name: `tile_count`: the real tiles of a slide stand first in its rows; some slide has no padding.
All inputs are finite; a program needn't handle non-finite values.
Results may differ from a plain program's by a relative error of at most 0.025.
Values may be sent and summed in bfloat16 or wider, within the bound.
A program may use at most 128 MiB of HBM per device.

v0:
```python
import jax
import jax.numpy as jnp
import numpy as np
from jax import lax
from jax.sharding import PartitionSpec as P

HEAD_WIDTH = 48
HEAD_TOTAL = 8
SEGMENT_FIRST = 1024
SEGMENT_SECOND = 4096
SEGMENT_THIRD = 16384
SEGMENT_FOURTH = 65536
DILATION_FIRST = 1
DILATION_SECOND = 4
DILATION_THIRD = 16
DILATION_FOURTH = 64


negative_large = -1e30
block_rows = 512


def as_sent(value):

    def short(part):
        return part.astype(jnp.bfloat16) if part.dtype == jnp.float32 else part

    return jax.tree.map(short, value)


def from_partner(value, axis, stride):
    return lax.ppermute(value, axis, [(i, i ^ 1 << stride) for i in range(lax.axis_size(axis))])


def apply_dilation(value_matrix, dilation_rate):
    head_number = value_matrix.shape[1]
    reshaped = value_matrix.reshape(
        (value_matrix.shape[0] // dilation_rate, dilation_rate) + value_matrix.shape[1:]
    )
    return reshaped[:, np.arange(head_number) % dilation_rate, np.arange(head_number)]


def reverse_dilation(value_matrix, dilation_rate, filler_value):
    head_number = value_matrix.shape[1]
    chosen_rows = (
        np.arange(dilation_rate)[:, None] == (np.arange(head_number) % dilation_rate)[None, :]
    )
    chosen_rows = chosen_rows.reshape(
        (1, dilation_rate, head_number) + (1,) * (value_matrix.ndim - 2)
    )
    spread_rows = jnp.where(chosen_rows, value_matrix[:, None], filler_value)
    return spread_rows.reshape((value_matrix.shape[0] * dilation_rate,) + value_matrix.shape[1:])


def split_blocks(value_matrix):
    segment_count, row_count = (value_matrix.shape[0], value_matrix.shape[1])
    step_rows = min(row_count, block_rows)
    reshaped = value_matrix.reshape(
        (segment_count, row_count // step_rows, step_rows) + value_matrix.shape[2:]
    )
    return jnp.moveaxis(reshaped, 1, 0)


def join_blocks(value_matrix):
    merged = jnp.moveaxis(value_matrix, 0, 1)
    return merged.reshape((merged.shape[0], merged.shape[1] * merged.shape[2]) + merged.shape[3:])


def live_mask(key_valid):
    return jnp.transpose(key_valid, (0, 2, 1))[:, :, None, :]


def per_head(value_matrix):
    return jnp.transpose(value_matrix, (0, 2, 1))[:, :, :, None]


def block_scores(query_blk, key_group, key_valid, scale_factor):
    raw_scores = (
        jnp.einsum("sqhd,skhd->shqk", query_blk, key_group, preferred_element_type=jnp.float32)
        * scale_factor
    )
    return jnp.where(live_mask(key_valid), raw_scores, negative_large)


def level_max(query_group, key_group, key_valid, scale_factor):

    def one_block(query_blk):
        return jnp.max(block_scores(query_blk, key_group, key_valid, scale_factor), axis=3)

    maxima = lax.map(one_block, split_blocks(query_group))
    return join_blocks(jnp.transpose(maxima, (0, 1, 3, 2)))


def level_totals(query_group, key_group, value_group, key_valid, row_maximum, scale_factor):
    live_grid = live_mask(key_valid)

    def one_block(block_parts):
        query_blk, max_blk = block_parts
        raw_scores = block_scores(query_blk, key_group, key_valid, scale_factor)
        expw = jnp.where(live_grid, jnp.exp(raw_scores - per_head(max_blk)), 0.0)
        weighted = jnp.einsum(
            "shqk,skhd->sqhd",
            expw.astype(jnp.bfloat16),
            value_group,
            preferred_element_type=jnp.float32,
        )
        return (jnp.transpose(jnp.sum(expw, axis=3), (0, 2, 1)), weighted)

    grand_totals, weighted = lax.map(
        one_block, (split_blocks(query_group), split_blocks(row_maximum))
    )
    return (join_blocks(grand_totals), join_blocks(weighted))


def level_back(
    query_group, gradient_group, key_group, value_group, key_valid, row_stats, scale_factor
):
    carry_start = (jnp.zeros(key_group.shape, jnp.float32), jnp.zeros(key_group.shape, jnp.float32))
    live_grid = live_mask(key_valid)

    def one_block(running, block_parts):
        query_blk, grad_blk, max_blk, den_blk, dot_blk = block_parts
        raw_scores = block_scores(query_blk, key_group, key_valid, scale_factor)
        prob_grid = jnp.where(live_grid, jnp.exp(raw_scores - per_head(max_blk)), 0.0) / per_head(
            den_blk
        )
        prob_grad = jnp.einsum(
            "sqhd,skhd->shqk", grad_blk, value_group, preferred_element_type=jnp.float32
        )
        score_grad = (prob_grid * (prob_grad - per_head(dot_blk))).astype(jnp.bfloat16)
        key_sum = (
            running[0]
            + jnp.einsum(
                "shqk,sqhd->skhd", score_grad, query_blk, preferred_element_type=jnp.float32
            )
            * scale_factor
        )
        value_sum = running[1] + jnp.einsum(
            "shqk,sqhd->skhd",
            prob_grid.astype(jnp.bfloat16),
            grad_blk,
            preferred_element_type=jnp.float32,
        )
        running = (key_sum, value_sum)
        query_part = (
            jnp.einsum("shqk,skhd->sqhd", score_grad, key_group, preferred_element_type=jnp.float32)
            * scale_factor
        )
        return (running, query_part)

    blocks = tuple(
        (
            split_blocks(statistic_rows)
            for statistic_rows in (query_group, gradient_group) + tuple(row_stats)
        )
    )
    final_keys, query_parts = lax.scan(one_block, carry_start, blocks)
    query_gradient = join_blocks(query_parts)
    return (query_gradient, final_keys[0], final_keys[1])


def send_keys(pieces, bit_pos):
    return jax.tree.map(
        lambda part, own: part.astype(own.dtype),
        from_partner(as_sent(pieces), "seq", bit_pos),
        pieces,
    )


def send_grads(pieces, bit_pos):
    return from_partner(pieces, "seq", bit_pos)


def doubling(pieces, group_width, sender, seq_index):
    gathered = pieces
    for bit_pos in range(group_width.bit_length() - 1):
        arrived = sender(gathered, bit_pos)
        upper_half = seq_index // 2**bit_pos % 2 == 1
        gathered = tuple(
            (
                jnp.where(
                    upper_half,
                    jnp.concatenate([far_rows, near_rows], 0),
                    jnp.concatenate([near_rows, far_rows], 0),
                )
                for near_rows, far_rows in zip(gathered, arrived)
            )
        )
    return gathered


def halving(pieces, group_width, sender, seq_index):
    current = pieces
    for bit_pos in reversed(range(group_width.bit_length() - 1)):
        half_rows = current[0].shape[0] // 2
        upper_half = seq_index // 2**bit_pos % 2 == 1
        kept_rows = tuple(
            (
                jnp.where(upper_half, piece_rows[half_rows:], piece_rows[:half_rows])
                for piece_rows in current
            )
        )
        given_rows = tuple(
            (
                jnp.where(upper_half, piece_rows[:half_rows], piece_rows[half_rows:])
                for piece_rows in current
            )
        )
        arrived = sender(given_rows, bit_pos)
        current = tuple((left_sum + right_sum for left_sum, right_sum in zip(kept_rows, arrived)))
    return current


def spanning_back(
    query_group,
    gradient_group,
    key_group,
    value_group,
    key_valid,
    row_stats,
    owned_keys,
    group_width,
    seq_index,
    scale_factor,
):
    dilation_rows, head_number, head_extent = owned_keys.shape
    total_width = head_number * head_extent
    broad_rows = group_width * dilation_rows
    level_pieces = level_back(
        query_group, gradient_group, key_group, value_group, key_valid, row_stats, scale_factor
    )
    summed_parts = halving(
        (
            level_pieces[1].reshape(broad_rows, total_width),
            level_pieces[2].reshape(broad_rows, total_width),
        ),
        group_width,
        send_grads,
        seq_index,
    )
    return (
        level_pieces[0],
        summed_parts[0].reshape(dilation_rows, head_number, head_extent),
        summed_parts[1].reshape(dilation_rows, head_number, head_extent),
    )


def local(tile_count, query_rows, key_rows, value_rows, out_grad, out_weight):
    local_tokens = query_rows.shape[0]
    head_number = HEAD_TOTAL
    head_extent = HEAD_WIDTH
    total_width = head_number * head_extent
    scale_factor = float(head_extent) ** (-0.5)
    seq_index = lax.axis_index("seq")
    seq_total = local_tokens * lax.axis_size("seq")
    tokens_total = seq_total * lax.axis_size("slide")
    first_row = seq_index * local_tokens
    local_count = tile_count[0]
    local_pos = first_row + jnp.arange(local_tokens, dtype=jnp.int32)
    query_live = (local_pos < local_count).astype(jnp.float32)
    head_position = jnp.broadcast_to(local_pos[:, None], (local_tokens, head_number))
    query_three = query_rows.reshape(local_tokens, head_number, head_extent)
    key_three = key_rows.reshape(local_tokens, head_number, head_extent)
    value_three = value_rows.reshape(local_tokens, head_number, head_extent)
    level_layouts = []
    for segment_length, dilation_rate in (
        (SEGMENT_FIRST, DILATION_FIRST),
        (SEGMENT_SECOND, DILATION_SECOND),
        (SEGMENT_THIRD, DILATION_THIRD),
        (SEGMENT_FOURTH, DILATION_FOURTH),
    ):
        seg_span = min(segment_length, seq_total)
        group_width = max(seg_span // local_tokens, 1)
        segment_count = max(local_tokens // seg_span, 1)
        dilation_rows = local_tokens // dilation_rate
        query_group = apply_dilation(query_three, dilation_rate).reshape(
            segment_count, dilation_rows // segment_count, head_number, head_extent
        )
        owned_keys = apply_dilation(key_three, dilation_rate)
        owned_values = apply_dilation(value_three, dilation_rate)
        owned_valid = apply_dilation(head_position, dilation_rate) < local_count
        joined_parts = doubling(
            (
                owned_keys.reshape(dilation_rows, total_width),
                owned_values.reshape(dilation_rows, total_width),
            ),
            group_width,
            send_keys,
            seq_index,
        )
        key_group = joined_parts[0].reshape(
            1, group_width * dilation_rows, head_number, head_extent
        )
        value_group = joined_parts[1].reshape(
            1, group_width * dilation_rows, head_number, head_extent
        )
        group_first = seq_index // group_width * (group_width * local_tokens)
        key_pos = (
            group_first
            + jnp.arange(group_width * dilation_rows, dtype=jnp.int32)[:, None] * dilation_rate
            + jnp.asarray(np.arange(head_number) % dilation_rate, jnp.int32)[None, :]
        )
        key_valid = (key_pos < local_count)[None]
        level_layouts.append(
            (
                dilation_rate,
                group_width,
                query_group,
                key_group,
                value_group,
                key_valid,
                owned_keys,
                owned_values,
                owned_valid,
            )
        )
    row_maximum = jnp.full((local_tokens, head_number), negative_large, jnp.float32)
    for level_layout in level_layouts:
        dilation_rate, group_width, query_group, key_group, value_group, key_valid = level_layout[
            :6
        ]
        level_peak = level_max(query_group, key_group, key_valid, scale_factor)
        row_maximum = jnp.maximum(
            row_maximum,
            reverse_dilation(level_peak.reshape(-1, head_number), dilation_rate, negative_large),
        )
    grand_totals = jnp.zeros((local_tokens, head_number), jnp.float32)
    summed_parts = jnp.zeros((local_tokens, head_number, head_extent), jnp.float32)
    for level_layout in level_layouts:
        dilation_rate, group_width, query_group, key_group, value_group, key_valid = level_layout[
            :6
        ]
        maximum_rows = apply_dilation(row_maximum, dilation_rate).reshape(query_group.shape[:3])
        level_pieces = level_totals(
            query_group, key_group, value_group, key_valid, maximum_rows, scale_factor
        )
        grand_totals = grand_totals + reverse_dilation(
            level_pieces[0].reshape(-1, head_number), dilation_rate, 0.0
        )
        summed_parts = summed_parts + reverse_dilation(
            level_pieces[1].reshape(-1, head_number, head_extent), dilation_rate, 0.0
        )
    row_denominator = grand_totals + (1.0 - query_live)[:, None]
    attended = (summed_parts / row_denominator[:, :, None] * query_live[:, None, None]).astype(
        jnp.bfloat16
    )
    attended_flat = attended.reshape(local_tokens, total_width)
    weight_local = jnp.einsum(
        "tc,td->cd", attended_flat, out_grad, preferred_element_type=jnp.float32
    )
    back_flat = (
        jnp.einsum("td,cd->tc", out_grad, out_weight, preferred_element_type=jnp.float32)
        * query_live[:, None]
    ).astype(jnp.bfloat16)
    backward_three = back_flat.reshape(local_tokens, head_number, head_extent)
    row_product = jnp.sum(backward_three.astype(jnp.float32) * attended.astype(jnp.float32), axis=2)
    query_gradient = jnp.zeros((local_tokens, head_number, head_extent), jnp.float32)
    key_gradient = jnp.zeros((local_tokens, head_number, head_extent), jnp.float32)
    value_gradient = jnp.zeros((local_tokens, head_number, head_extent), jnp.float32)
    for level_layout in level_layouts:
        (
            dilation_rate,
            group_width,
            query_group,
            key_group,
            value_group,
            key_valid,
            owned_keys,
            owned_values,
            owned_valid,
        ) = level_layout
        row_stats = tuple(
            (
                apply_dilation(statistic_rows, dilation_rate).reshape(query_group.shape[:3])
                for statistic_rows in (row_maximum, row_denominator, row_product)
            )
        )
        gradient_group = apply_dilation(backward_three, dilation_rate).reshape(query_group.shape)
        level_pieces = spanning_back(
            query_group,
            gradient_group,
            key_group,
            value_group,
            key_valid,
            row_stats,
            owned_keys,
            group_width,
            seq_index,
            scale_factor,
        )
        query_gradient = query_gradient + reverse_dilation(
            level_pieces[0].reshape(-1, head_number, head_extent), dilation_rate, 0.0
        )
        key_gradient = key_gradient + reverse_dilation(
            level_pieces[1].reshape(-1, head_number, head_extent), dilation_rate, 0.0
        )
        value_gradient = value_gradient + reverse_dilation(
            level_pieces[2].reshape(-1, head_number, head_extent), dilation_rate, 0.0
        )
    weight_grad = lax.psum(weight_local, ("slide", "seq")) * float(tokens_total) ** (-0.5)
    return (
        query_gradient.reshape(local_tokens, total_width).astype(jnp.bfloat16),
        key_gradient.reshape(local_tokens, total_width).astype(jnp.bfloat16),
        value_gradient.reshape(local_tokens, total_width).astype(jnp.bfloat16),
        weight_grad,
    )


def solution(mesh):
    in_specs = (
        P("slide"),
        P(("slide", "seq"), None),
        P(("slide", "seq"), None),
        P(("slide", "seq"), None),
        P(("slide", "seq"), None),
        P(),
    )
    out_specs = (
        P(("slide", "seq"), None),
        P(("slide", "seq"), None),
        P(("slide", "seq"), None),
        P(),
    )
    return jax.shard_map(local, mesh=mesh, in_specs=in_specs, out_specs=out_specs, check_vma=False)
```

profile of v0, /device:TPU:1, one launch (start us, length us, event | category | flops | bytes accessed | tf_op | source)
XLA Modules:
  0.0 652.1 jit_solution(10221183163893520511)
XLA Ops:
  54.0 3.5 copy.747
  68.0 3.0 copy.731
  85.4 3.0 copy.853
  99.6 3.1 collective-permute-start.24
  136.6 3.5 collective-permute-start.27
  144.1 3.2 collective-permute-start.2
  182.3 8.4 %fusion = (f32[8,512]{1,0:T(8,128)S(1)}, f32[8,512,1024]{2,1,0:T(8,128)}) fusion(pred[1024]{0:T(1024)(128)(4,1)} %add_compare_fusion.3, bf16[512,8,48]{0,2,1:T(8,128)(2,1)S(1)} %bitcast.516, bf16[512,8,48]{0,2,1:T(8,128)(2,1)} %bitcast.3, pred[]{:T(512)S(6)} %eq.67, bf16[8,512,48]{1,2,0:T(8,128)(2,1)S(1)} %gather_fusion.1), kind=kOutput, calls=%fused_computation.31 | convolution fusion | flops 418770944 | bytes 17974272 | tf_op jit(solution)/shard_map/while/body/eval_jaxpr/sqhd,skhd->shqk/dot_general | solution.py:79
  191.9 4.5 fusion.5
  202.1 8.2 %fusion.10 = f32[8,512]{1,0:T(8,128)S(1)} fusion(f32[8,512]{1,0:T(8,128)S(1)} %gather_fusion.8, f32[8,512,1024]{2,1,0:T(8,128)} %get-tuple-element.334, pred[1024]{0:T(1024)(128)(4,1)S(1)} %copy-done.112), kind=kLoop, calls=%fused_computation.58 | loop fusion | flops 20967424 | bytes 16811008 | tf_op jit(solution)/shard_map/while/body/eval_jaxpr/reduce_sum | solution.py:107
  214.3 3.5 fusion.63
  229.0 4.5 fusion.22
  243.1 3.1 copy.805
  248.7 10.3 %fusion.52 = (f32[512,8]{0,1:T(8,128)S(1)}, f32[8,48,512]{2,1,0:T(8,128)}) fusion(bf16[512,8,48]{0,2,1:T(8,128)(2,1)S(1)} %bitcast.510, f32[512]{0:T(512)} %copy-done.107, f32[512,8]{0,1:T(8,128)S(1)} %fusion.95, f32[512,8,48]{0,2,1:T(8,128)} %broadcast_in_dim.1246, pred[512,8]{0,1:T(8,128)(4,1)} %broadcast_in_dim.1240, f32[512,8,48]{0,2,1:T(8,128)} %copy.805, ...), kind=kOutput, calls=%fused_computation.120 | convolution fusion | flops 429715456 | bytes 21167104 | tf_op jit(solution)/shard_map/while/body/eval_jaxpr/shqk,skhd->sqhd/dot_general | solution.py:101
  262.0 4.9 fusion.14
  266.9 3.1 multiply_convert_fusion.1
  285.9 10.1 %fusion.11 = f32[1,1024,8,48]{1,3,2,0:T(8,128)} fusion(f32[8,512]{1,0:T(8,128)S(1)} %gather_fusion.12, f32[8,512]{1,0:T(8,128)S(1)} %copy-done.13, f32[8,512,1024]{2,1,0:T(8,128)} %get-tuple-element.334, pred[1024]{0:T(1024)(128)(4,1)S(1)} %copy-done.113, bf16[8,512,48]{1,2,0:T(8,128)(2,1)S(1)} %copy-done.21), kind=kOutput, calls=%fused_computation.62 | convolution fusion | flops 427819008 | bytes 18777088 | tf_op jit(solution)/shard_map/while/body/eval_jaxpr/shqk,sqhd->skhd/dot_general | solution.py:138
  296.0 10.6 %multiply_convert_fusion = bf16[8,512,1024]{2,1,0:T(8,128)(2,1)S(1)} fusion(f32[8,512]{1,0:T(8,128)S(1)} %gather_fusion.18, f32[8,512]{1,0:T(8,128)S(1)} %gather_fusion.12, f32[8,512]{1,0:T(8,128)S(1)} %copy-done.13, f32[8,512,1024]{2,1,0:T(8,128)} %get-tuple-element.334, pred[1024]{0:T(1024)(128)(4,1)S(1)} %copy-done.113, ...), kind=kOutput, calls=%fused_computation.28 | convolution fusion | flops 439746560 | bytes 26395648 | tf_op jit(solution)/shard_map/while/body/eval_jaxpr/sqhd,skhd->shqk/dot_general | solution.py:127
  306.6 4.7 convolution_multiply_fusion.1
  346.0 5.4 collective-permute-done.37
  352.9 5.6 collective-permute-done.52
  360.1 4.8 collective-permute-done.38
  366.3 5.6 collective-permute-done.53
  373.4 3.2 collective-permute-done.39
  396.7 3.3 collective-permute-done.41
  400.0 3.2 collective-permute-start.32
  409.4 4.2 collective-permute-start.44
  418.6 9.9 %collective-permute-done.44 = f32[256,384]{0,1:T(8,128)S(1)} collective-permute-done((f32[256,384]{0,1:T(8,128)S(1)}, f32[256,384]{0,1:T(8,128)S(1)}, u32[]{:S(2)}, u32[]{:S(2)}) %collective-permute-start.44) | collective-permute-done | bytes 393248 | tf_op jit(solution)/shard_map/ppermute | solution.py:32
  429.8 3.4 collective-permute-done.30
  437.2 3.1 collective-permute-done.45
  451.5 4.7 collective-permute-done.35
  462.0 5.9 fusion.54
  487.1 155.3 %all-reduce.2.cloned.1.call-done = f32[384,768]{1,0:T(8,128)} async-done(((f32[384,768]{1,0:T(8,128)}), f32[384,768]{1,0:T(8,128)}) %all-reduce.2.cloned.1.call-update) | async-done | bytes 1179664 | tf_op jit(solution)/shard_map/psum | solution.py:400
  (664 shorter events, 321.4 us)
Async XLA Ops:
  7.2 635.2 %all-reduce.2.cloned.1.call-start = ((), (), s32[]{:S(2)}) async-start(), calls=%async_computation | async-start | bytes 2359296 | tf_op jit(solution)/shard_map/psum | solution.py:400
  11.8 86.9 %collective-permute-start.23 = (bf16[8,384]{1,0:T(8,128)(2,1)}, bf16[8,384]{1,0:T(8,128)(2,1)}, u32[]{:S(2)}, u32[]{:S(2)}) collective-permute-start(bf16[8,384]{1,0:T(8,128)(2,1)} %reshape.1402), channel_id=1, source_target_pairs={{0,1},{1,0},{2,3},{3,2},{4,5},{5,4},{6,7},{7,6},{8,9},{9,8},{10,11... | collective-permute-start | bytes 18440 | tf_op jit(solution)/shard_map/ppermute | solution.py:32
  18.4 81.2 %collective-permute-start.9 = (bf16[8,384]{1,0:T(8,128)(2,1)}, bf16[8,384]{1,0:T(8,128)(2,1)}, u32[]{:S(2)}, u32[]{:S(2)}) collective-permute-start(bf16[8,384]{1,0:T(8,128)(2,1)} %reshape.1398), channel_id=1, source_target_pairs={{0,1},{1,0},{2,3},{3,2},{4,5},{5,4},{6,7},{7,6},{8,9},{9,8},{10,11... | collective-permute-start | bytes 18440 | tf_op jit(solution)/shard_map/ppermute | solution.py:32
  19.3 162.5 %collective-permute-start = (bf16[512,384]{0,1:T(8,128)(2,1)S(1)}, bf16[512,384]{0,1:T(8,128)(2,1)}, u32[]{:S(2)}, u32[]{:S(2)}) collective-permute-start(bf16[512,384]{0,1:T(8,128)(2,1)S(1)} %bitcast.515), channel_id=1, source_target_pairs={{0,1},{1,0},{2,3},{3,2},{4,5},{5,4},{6,7},{7,6},{8,9},{9,8},{10,11... | collective-permute-start | bytes 1179656 | tf_op jit(solution)/shard_map/ppermute | solution.py:32
  25.9 83.5 %collective-permute-start.4 = (bf16[32,384]{1,0:T(8,128)(2,1)}, bf16[32,384]{1,0:T(8,128)(2,1)}, u32[]{:S(2)}, u32[]{:S(2)}) collective-permute-start(bf16[32,384]{1,0:T(8,128)(2,1)} %reshape.1397), channel_id=1, source_target_pairs={{0,1},{1,0},{2,3},{3,2},{4,5},{5,4},{6,7},{7,6},{8,9},{9,8},{10,11... | collective-permute-start | bytes 73736 | tf_op jit(solution)/shard_map/ppermute | solution.py:32
  29.2 106.1 %collective-permute-start.1 = (bf16[128,384]{0,1:T(8,128)(2,1)}, bf16[128,384]{0,1:T(8,128)(2,1)}, u32[]{:S(2)}, u32[]{:S(2)}) collective-permute-start(bf16[128,384]{0,1:T(8,128)(2,1)} %bitcast.14), channel_id=1, source_target_pairs={{0,1},{1,0},{2,3},{3,2},{4,5},{5,4},{6,7},{7,6},{8,9},{9,8},{10,11... | collective-permute-start | bytes 294920 | tf_op jit(solution)/shard_map/ppermute | solution.py:32
  98.7 11.8 %collective-permute-start.18 = (bf16[32,384]{1,0:T(8,128)(2,1)S(1)}, bf16[32,384]{1,0:T(8,128)(2,1)S(1)}, u32[]{:S(2)}, u32[]{:S(2)}) collective-permute-start(bf16[32,384]{1,0:T(8,128)(2,1)S(1)} %copy-done.79), channel_id=1, source_target_pairs={{0,1},{1,0},{2,3},{3,2},{4,5},{5,4},{6,7},{7,6},{8,9},{9,8},{10,11... | collective-permute-start | bytes 73736 | tf_op jit(solution)/shard_map/ppermute | solution.py:32
  107.9 28.7 %collective-permute-start.15 = (bf16[128,384]{0,1:T(8,128)(2,1)S(1)}, bf16[128,384]{0,1:T(8,128)(2,1)S(1)}, u32[]{:S(2)}, u32[]{:S(2)}) collective-permute-start(bf16[128,384]{0,1:T(8,128)(2,1)S(1)} %bitcast.524), channel_id=1, source_target_pairs={{0,1},{1,0},{2,3},{3,2},{4,5},{5,4},{6,7},{7,6},{8,9},{9,8},{10,11... | collective-permute-start | bytes 294920 | tf_op jit(solution)/shard_map/ppermute | solution.py:32
  109.5 139.1 %collective-permute-start.14 = (bf16[512,384]{0,1:T(8,128)(2,1)}, bf16[512,384]{0,1:T(8,128)(2,1)}, u32[]{:S(2)}, u32[]{:S(2)}) collective-permute-start(bf16[512,384]{0,1:T(8,128)(2,1)} %bitcast.71), channel_id=1, source_target_pairs={{0,1},{1,0},{2,3},{3,2},{4,5},{5,4},{6,7},{7,6},{8,9},{9,8},{10,11... | collective-permute-start | bytes 1179656 | tf_op jit(solution)/shard_map/ppermute | solution.py:32
  131.8 10.5 %collective-permute-start.6 = (bf16[128,384]{1,0:T(8,128)(2,1)S(1)}, bf16[128,384]{1,0:T(8,128)(2,1)S(1)}, u32[]{:S(2)}, u32[]{:S(2)}) collective-permute-start(bf16[128,384]{1,0:T(8,128)(2,1)S(1)} %maximum_select_fusion.36), channel_id=1, source_target_pairs={{0,4},{1,5},{2,6},{3,7},{4,0},{5,1},{6,2},{7,3},{8,12},{9,13},{10,... | collective-permute-start | bytes 294920 | tf_op jit(solution)/shard_map/ppermute | solution.py:32
  136.6 22.6 %collective-permute-start.27 = (bf16[128,384]{1,0:T(8,128)(2,1)}, bf16[128,384]{1,0:T(8,128)(2,1)}, u32[]{:S(2)}, u32[]{:S(2)}) collective-permute-start(bf16[128,384]{1,0:T(8,128)(2,1)} %maximum_select_fusion.44), channel_id=1, source_target_pairs={{0,16},{1,17},{2,18},{3,19},{4,20},{5,21},{6,22},{7,23},{8,24},{9,... | collective-permute-start | bytes 294920 | tf_op jit(solution)/shard_map/ppermute | solution.py:32
  144.1 17.5 %collective-permute-start.2 = (bf16[256,384]{0,1:T(8,128)(2,1)S(1)}, bf16[256,384]{0,1:T(8,128)(2,1)}, u32[]{:S(2)}, u32[]{:S(2)}) collective-permute-start(bf16[256,384]{0,1:T(8,128)(2,1)S(1)} %maximum_select_fusion.14), channel_id=1, source_target_pairs={{0,2},{1,3},{2,0},{3,1},{4,6},{5,7},{6,4},{7,5},{8,10},{9,11},{10,... | collective-permute-start | bytes 589832 | tf_op jit(solution)/shard_map/ppermute | solution.py:32
  151.3 14.8 %collective-permute-start.16 = (bf16[256,384]{0,1:T(8,128)(2,1)S(1)}, bf16[256,384]{0,1:T(8,128)(2,1)}, u32[]{:S(2)}, u32[]{:S(2)}) collective-permute-start(bf16[256,384]{0,1:T(8,128)(2,1)S(1)} %maximum_select_fusion.19), channel_id=1, source_target_pairs={{0,2},{1,3},{2,0},{3,1},{4,6},{5,7},{6,4},{7,5},{8,10},{9,11},{10,... | collective-permute-start | bytes 589832 | tf_op jit(solution)/shard_map/ppermute | solution.py:32
  159.2 11.8 %collective-permute-start.7 = (bf16[256,384]{1,0:T(8,128)(2,1)}, bf16[256,384]{1,0:T(8,128)(2,1)}, u32[]{:S(2)}, u32[]{:S(2)}) collective-permute-start(bf16[256,384]{1,0:T(8,128)(2,1)} %maximum_select_fusion.16), channel_id=1, source_target_pairs={{0,8},{1,9},{2,10},{3,11},{4,12},{5,13},{6,14},{7,15},{8,0},{9,1},... | collective-permute-start | bytes 589832 | tf_op jit(solution)/shard_map/ppermute | solution.py:32
  161.6 13.0 %collective-permute-start.21 = (bf16[256,384]{1,0:T(8,128)(2,1)S(1)}, bf16[256,384]{1,0:T(8,128)(2,1)}, u32[]{:S(2)}, u32[]{:S(2)}) collective-permute-start(bf16[256,384]{1,0:T(8,128)(2,1)S(1)} %maximum_select_fusion.21), channel_id=1, source_target_pairs={{0,8},{1,9},{2,10},{3,11},{4,12},{5,13},{6,14},{7,15},{8,0},{9,1},... | collective-permute-start | bytes 589832 | tf_op jit(solution)/shard_map/ppermute | solution.py:32
  166.1 25.8 %collective-permute-start.3 = (bf16[512,384]{0,1:T(8,128)(2,1)}, bf16[512,384]{0,1:T(8,128)(2,1)}, u32[]{:S(2)}, u32[]{:S(2)}) collective-permute-start(bf16[512,384]{0,1:T(8,128)(2,1)} %maximum_select_fusion.6), channel_id=1, source_target_pairs={{0,4},{1,5},{2,6},{3,7},{4,0},{5,1},{6,2},{7,3},{8,12},{9,13},{10,... | collective-permute-start | bytes 1179656 | tf_op jit(solution)/shard_map/ppermute | solution.py:32
  171.0 58.0 %collective-permute-start.17 = (bf16[512,384]{0,1:T(8,128)(2,1)}, bf16[512,384]{0,1:T(8,128)(2,1)}, u32[]{:S(2)}, u32[]{:S(2)}) collective-permute-start(bf16[512,384]{0,1:T(8,128)(2,1)} %maximum_select_fusion.10), channel_id=1, source_target_pairs={{0,4},{1,5},{2,6},{3,7},{4,0},{5,1},{6,2},{7,3},{8,12},{9,13},{10,... | collective-permute-start | bytes 1179656 | tf_op jit(solution)/shard_map/ppermute | solution.py:32
  174.6 21.8 %collective-permute-start.8 = (bf16[512,384]{1,0:T(8,128)(2,1)}, bf16[512,384]{1,0:T(8,128)(2,1)S(1)}, u32[]{:S(2)}, u32[]{:S(2)}) collective-permute-start(bf16[512,384]{1,0:T(8,128)(2,1)} %maximum_select_fusion.8), channel_id=1, source_target_pairs={{0,16},{1,17},{2,18},{3,19},{4,20},{5,21},{6,22},{7,23},{8,24},{9,... | collective-permute-start | bytes 1179656 | tf_op jit(solution)/shard_map/ppermute | solution.py:32
  181.8 42.2 %collective-permute-start.22 = (bf16[512,384]{1,0:T(8,128)(2,1)}, bf16[512,384]{1,0:T(8,128)(2,1)}, u32[]{:S(2)}, u32[]{:S(2)}) collective-permute-start(bf16[512,384]{1,0:T(8,128)(2,1)} %maximum_select_fusion.12), channel_id=1, source_target_pairs={{0,16},{1,17},{2,18},{3,19},{4,20},{5,21},{6,22},{7,23},{8,24},{9,... | collective-permute-start | bytes 1179656 | tf_op jit(solution)/shard_map/ppermute | solution.py:32
  328.5 15.1 %collective-permute-start.51 = (f32[128,384]{0,1:T(8,128)S(1)}, f32[128,384]{0,1:T(8,128)S(1)}, u32[]{:S(2)}, u32[]{:S(2)}) collective-permute-start(f32[128,384]{0,1:T(8,128)S(1)} %bitcast.569), channel_id=1, source_target_pairs={{0,16},{1,17},{2,18},{3,19},{4,20},{5,21},{6,22},{7,23},{8,24},{9,... | collective-permute-start | bytes 589832 | tf_op jit(solution)/shard_map/ppermute | solution.py:32
  333.9 72.1 %collective-permute-start.46 = (f32[512,384]{0,1:T(8,128)}, f32[512,384]{0,1:T(8,128)}, u32[]{:S(2)}, u32[]{:S(2)}) collective-permute-start(f32[512,384]{0,1:T(8,128)} %bitcast.170), channel_id=1, source_target_pairs={{0,16},{1,17},{2,18},{3,19},{4,20},{5,21},{6,22},{7,23},{8,24},{9,... | collective-permute-start | bytes 2359304 | tf_op jit(solution)/shard_map/ppermute | solution.py:32
  336.1 71.6 %collective-permute-start.43 = (f32[512,384]{0,1:T(8,128)}, f32[512,384]{0,1:T(8,128)}, u32[]{:S(2)}, u32[]{:S(2)}) collective-permute-start(f32[512,384]{0,1:T(8,128)} %bitcast.164), channel_id=1, source_target_pairs={{0,4},{1,5},{2,6},{3,7},{4,0},{5,1},{6,2},{7,3},{8,12},{9,13},{10,... | collective-permute-start | bytes 2359304 | tf_op jit(solution)/shard_map/ppermute | solution.py:32
  338.7 123.3 %collective-permute-start.42 = (f32[512,384]{0,1:T(8,128)}, f32[512,384]{0,1:T(8,128)}, u32[]{:S(2)}, u32[]{:S(2)}) collective-permute-start(f32[512,384]{0,1:T(8,128)} %bitcast.159), channel_id=1, source_target_pairs={{0,1},{1,0},{2,3},{3,2},{4,5},{5,4},{6,7},{7,6},{8,9},{9,8},{10,11... | collective-permute-start | bytes 2359304 | tf_op jit(solution)/shard_map/ppermute | solution.py:32
  340.8 68.6 %collective-permute-start.29 = (f32[512,384]{0,1:T(8,128)}, f32[512,384]{0,1:T(8,128)}, u32[]{:S(2)}, u32[]{:S(2)}) collective-permute-start(f32[512,384]{0,1:T(8,128)} %bitcast.141), channel_id=1, source_target_pairs={{0,4},{1,5},{2,6},{3,7},{4,0},{5,1},{6,2},{7,3},{8,12},{9,13},{10,... | collective-permute-start | bytes 2359304 | tf_op jit(solution)/shard_map/ppermute | solution.py:32
  400.0 14.9 %collective-permute-start.32 = (f32[512,384]{0,1:T(8,128)}, f32[512,384]{0,1:T(8,128)}, u32[]{:S(2)}, u32[]{:S(2)}) collective-permute-start(f32[512,384]{0,1:T(8,128)} %bitcast.539), channel_id=1, source_target_pairs={{0,16},{1,17},{2,18},{3,19},{4,20},{5,21},{6,22},{7,23},{8,24},{9,... | collective-permute-start | bytes 2359304 | tf_op jit(solution)/shard_map/ppermute | solution.py:32
  406.1 76.9 %collective-permute-start.28 = (f32[512,384]{0,1:T(8,128)}, f32[512,384]{0,1:T(8,128)}, u32[]{:S(2)}, u32[]{:S(2)}) collective-permute-start(f32[512,384]{0,1:T(8,128)} %bitcast.538), channel_id=1, source_target_pairs={{0,1},{1,0},{2,3},{3,2},{4,5},{5,4},{6,7},{7,6},{8,9},{9,8},{10,11... | collective-permute-start | bytes 2359304 | tf_op jit(solution)/shard_map/ppermute | solution.py:32
  407.7 9.6 %collective-permute-start.47 = (f32[256,384]{0,1:T(8,128)S(1)}, f32[256,384]{0,1:T(8,128)S(1)}, u32[]{:S(2)}, u32[]{:S(2)}) collective-permute-start(f32[256,384]{0,1:T(8,128)S(1)} %slice_select_fusion.12), channel_id=1, source_target_pairs={{0,8},{1,9},{2,10},{3,11},{4,12},{5,13},{6,14},{7,15},{8,0},{9,1},... | collective-permute-start | bytes 1179656 | tf_op jit(solution)/shard_map/ppermute | solution.py:32
  409.4 19.1 %collective-permute-start.44 = (f32[256,384]{0,1:T(8,128)S(1)}, f32[256,384]{0,1:T(8,128)S(1)}, u32[]{:S(2)}, u32[]{:S(2)}) collective-permute-start(f32[256,384]{0,1:T(8,128)S(1)} %slice_select_fusion.13), channel_id=1, source_target_pairs={{0,2},{1,3},{2,0},{3,1},{4,6},{5,7},{6,4},{7,5},{8,10},{9,11},{10,... | collective-permute-start | bytes 1179656 | tf_op jit(solution)/shard_map/ppermute | solution.py:32
  414.9 18.3 %collective-permute-start.30 = (f32[256,384]{0,1:T(8,128)S(1)}, f32[256,384]{0,1:T(8,128)S(1)}, u32[]{:S(2)}, u32[]{:S(2)}) collective-permute-start(f32[256,384]{0,1:T(8,128)S(1)} %slice_select_fusion.15), channel_id=1, source_target_pairs={{0,2},{1,3},{2,0},{3,1},{4,6},{5,7},{6,4},{7,5},{8,10},{9,11},{10,... | collective-permute-start | bytes 1179656 | tf_op jit(solution)/shard_map/ppermute | solution.py:32
  417.3 16.8 %collective-permute-start.33 = (f32[256,384]{0,1:T(8,128)S(1)}, f32[256,384]{0,1:T(8,128)S(1)}, u32[]{:S(2)}, u32[]{:S(2)}) collective-permute-start(f32[256,384]{0,1:T(8,128)S(1)} %slice_select_fusion.14), channel_id=1, source_target_pairs={{0,8},{1,9},{2,10},{3,11},{4,12},{5,13},{6,14},{7,15},{8,0},{9,1},... | collective-permute-start | bytes 1179656 | tf_op jit(solution)/shard_map/ppermute | solution.py:32
  434.1 36.7 %collective-permute-start.31 = (f32[128,384]{0,1:T(8,128)}, f32[128,384]{0,1:T(8,128)}, u32[]{:S(2)}, u32[]{:S(2)}) collective-permute-start(f32[128,384]{0,1:T(8,128)} %slice_select_fusion.35), channel_id=1, source_target_pairs={{0,1},{1,0},{2,3},{3,2},{4,5},{5,4},{6,7},{7,6},{8,9},{9,8},{10,11... | collective-permute-start | bytes 589832 | tf_op jit(solution)/shard_map/ppermute | solution.py:32
  440.3 9.9 %collective-permute-start.49 = (f32[64,384]{0,1:T(8,128)S(1)}, f32[64,384]{0,1:T(8,128)}, u32[]{:S(2)}, u32[]{:S(2)}) collective-permute-start(f32[64,384]{0,1:T(8,128)S(1)} %slice_select_fusion.23), channel_id=1, source_target_pairs={{0,2},{1,3},{2,0},{3,1},{4,6},{5,7},{6,4},{7,5},{8,10},{9,11},{10,... | collective-permute-start | bytes 294920 | tf_op jit(solution)/shard_map/ppermute | solution.py:32
  (141 other events, 1948.5 us)
Sparse Core Ops, SparseCore 0:
  469.5 172.8 all-reduce.1
where the time goes:
time: 662 us; the launch traced here: 652 us
  waiting for transfers between devices  222 us (34%)
  local copies, waits for them, and re-layouts  164 us (25%)
  other arithmetic  85.9 us (13%)
  matrix products  83.6 us (13%)
  starting transfers between devices  78.8 us (12%)
  between operations  17.6 us (3%)
    psum x1, waiting for transfers between devices, local(): lax.psum(weight_local, ('slide', 'seq')) * float(tokens_total) ** (-0.5)  155 us
    ppermute x56, starting transfers between devices, from_partner(): lax.ppermute(value, axis, [(i, i ^ 1 << stride) for i in range(lax.axis_s...  78.7 us
    ppermute x56, waiting for transfers between devices, from_partner(): lax.ppermute(value, axis, [(i, i ^ 1 << stride) for i in range(lax.axis_s...  66.9 us
    broadcast_in_dim x71, local copies, waits for them, and re-layouts, reverse_dilation(): spread_rows = jnp.where(chosen_rows, value_matrix[:, None], filler_value)  58.1 us
    another operation x24, local copies, waits for them, and re-layouts, apply_dilation(): value_matrix.reshape((value_matrix.shape[0] // dilation_rate, dilation_ra...  47.8 us
    gather x32, local copies, waits for them, and re-layouts, apply_dilation(): reshaped[:, np.arange(head_number) % dilation_rate, np.arange(head_number)]  29.5 us
    select_n x36, other arithmetic, doubling(): jnp.where(upper_half, jnp.concatenate([far_rows, near_rows], 0), jnp.conc...  28.6 us
    dot_general x4, matrix products, one_block(): jnp.einsum('shqk,sqhd->skhd', prob_grid.astype(jnp.bfloat16), grad_blk, p...  17.7 us
  transfers between devices with their start and end apart: 57, of which 23 were waited for; matrix products, arithmetic and copies ran while one was open for 38% of the time, Pallas kernels for 0%

commit v1 on v0

v1 whole, which is shorter than its diff:
```python
import jax
import jax.numpy as jnp
from jax import lax
from jax.experimental import pallas as pl
from jax.experimental.pallas import tpu as pltpu
from jax.sharding import PartitionSpec as P

HEAD_WIDTH = 48
HEADS = 8
ROWS = 512
SPAN = 4096
WIDTH = 384
DEPTH = 768
PLANES = 4
LANES_ALL = 6144
LANES_QUERY = 5376
BLOCK = 256
BLOCKS = LANES_QUERY // BLOCK
DEAD = -1e30
SCALE = float(HEAD_WIDTH) ** -0.5
SCALE_TWO = SCALE * 1.4426950408889634
BF = jnp.bfloat16
F32 = jnp.float32
VMEM_LIMIT = 56 * 1024 * 1024


def dot(lhs, rhs):
    return jnp.dot(lhs, rhs, preferred_element_type=F32)


def dot_nt(lhs, rhs):
    return lax.dot_general(lhs, rhs, (((1,), (1,)), ((), ())), preferred_element_type=F32)


def row_of(slot, swap):
    a, b, c, d = slot // 128, slot // 32 % 4, slot // 8 % 4, slot % 8
    b = jnp.where(b < 2, jnp.where(swap, 1 - b, b), b)
    return a + 4 * b + 16 * c + 64 * d


def order_matrix(swap):
    rows = lax.broadcasted_iota(jnp.int32, (ROWS, ROWS), 0)
    slots = lax.broadcasted_iota(jnp.int32, (ROWS, ROWS), 1)
    return jnp.where(rows == row_of(slots, swap), 1.0, 0.0).astype(BF)


def place():
    seq = lax.axis_index("seq")
    return seq // HEADS, seq % HEADS


def enter(plane, head):
    barrier = pltpu.get_barrier_semaphore()
    for step in range(1, HEADS):
        peer = plane * HEADS + (head + step) % HEADS
        pl.semaphore_signal(
            barrier, inc=1, device_id={"seq": peer}, device_id_type=pl.DeviceIdType.MESH
        )
    for step in range(1, PLANES):
        peer = (plane + step) % PLANES * HEADS + head
        pl.semaphore_signal(
            barrier, inc=1, device_id={"seq": peer}, device_id_type=pl.DeviceIdType.MESH
        )
    pl.semaphore_wait(barrier, HEADS + PLANES - 2)


def remote(src, dst, send_sem, recv_sem, peer):
    return pltpu.make_async_remote_copy(
        src_ref=src,
        dst_ref=dst,
        send_sem=send_sem,
        recv_sem=recv_sem,
        device_id={"seq": peer},
        device_id_type=pl.DeviceIdType.MESH,
    )


def spread_kernel(
    count_ref,
    query_ref,
    key_ref,
    value_ref,
    grad_ref,
    weight_ref,
    land_ref,
    far_ref,
    send,
    far_send,
    send_sem,
    recv_sem,
    own_sem,
    far_send_sem,
    far_recv_sem,
    far_own_sem,
):
    plane, head = place()
    orders = (order_matrix(False), order_matrix(True))

    def stage(part, value_t):
        for half in range(2):
            moved = dot(value_t[192 * half : 192 * half + 192], orders[half]).astype(BF)
            for turn in range(4):
                rows = moved[48 * turn : 48 * turn + 48]
                if turn:
                    rows = jnp.concatenate([rows[:, 128 * turn :], rows[:, : 128 * turn]], axis=1)
                send[4 * half + turn, 48 * part : 48 * part + 48, :] = rows

    def launch(group, first, last):
        copies = []
        for step in range(1, HEADS):
            to = (head + step) % HEADS
            copy = remote(
                send.at[to, first:last],
                land_ref.at[head, first:last],
                send_sem.at[group, step],
                recv_sem.at[group, step],
                plane * HEADS + to,
            )
            copy.start()
            copies.append(copy)
        own = pltpu.make_async_copy(
            send.at[head, first:last], land_ref.at[head, first:last], own_sem.at[group]
        )
        own.start()
        copies.append(own)
        return copies

    stage(1, key_ref[...].T)
    stage(0, query_ref[...].T)
    enter(plane, head)
    first = launch(0, 0, 96)
    stage(2, value_ref[...].T)
    second = launch(1, 96, 144)
    lane = lax.broadcasted_iota(jnp.int32, (1, ROWS), 1)
    live = (plane * SPAN + head * ROWS + lane < count_ref[0]).astype(F32)
    back = (dot_nt(weight_ref[...], grad_ref[...]) * live).astype(BF)
    stage(3, back)
    third = launch(2, 144, 192)
    for copy in first + second:
        copy.wait()
    tiles = jnp.concatenate([land_ref[s, 48:144, 0:128] for s in range(HEADS)], axis=1)
    here = lax.broadcasted_iota(jnp.int32, (1024, 256), 0)
    there = lax.broadcasted_iota(jnp.int32, (1024, 256), 1)
    pick = jnp.where(here == there // 32 * 128 + there % 32, 1.0, 0.0).astype(BF)
    far_send[...] = dot(tiles, pick).astype(BF)
    copies = []
    for step in range(1, PLANES):
        copy = remote(
            far_send,
            far_ref.at[plane],
            far_send_sem.at[step],
            far_recv_sem.at[step],
            (plane + step) % PLANES * HEADS + head,
        )
        copy.start()
        copies.append(copy)
    own = pltpu.make_async_copy(far_send, far_ref.at[plane], far_own_sem)
    own.start()
    for copy in third + copies + [own]:
        copy.wait()


def spread_tiles(value, s):
    tile = value[:, 128 * (s // 4) : 128 * (s // 4) + 128]
    shift = (128 - 32 * (s % 4)) % 128
    return pltpu.roll(tile, shift, 1) if shift else tile


def attend_kernel(
    count_ref,
    land_ref,
    far_ref,
    att_ref,
    out_ref,
    far_out_ref,
    all_t,
    query_a,
    key_a,
    value_a,
    value_t,
    stats,
    outs,
    probs,
    grad_a,
    right,
    sums,
):
    plane, head = place()
    count = count_ref[0]
    for s in range(HEADS):
        all_t[:, 512 * s : 512 * s + 512] = land_ref[s]
        all_t[:, 4096 + 128 * s : 4096 + 128 * s + 128] = land_ref[s, :, 0:128]
    here = lax.broadcasted_iota(jnp.int32, (1024, 256), 0)
    there = lax.broadcasted_iota(jnp.int32, (1024, 256), 1)
    pick = jnp.where(here == there // 32 * 128 + there % 32, 1.0, 0.0).astype(BF)
    packed = dot(all_t[:, 4096:5120], pick).astype(BF)
    all_t[0:48, 5120:5376] = packed[0:48]
    all_t[144:192, 5120:5376] = packed[144:192]
    for z in range(PLANES):
        all_t[48:144, 5120 + 256 * z : 5376 + 256 * z] = far_ref[z]

    lane = lax.broadcasted_iota(jnp.int32, (1, LANES_ALL), 1)
    near = lane - 4096
    far = lane - 5120
    block = jnp.where(lane < 4096, lane // 512, jnp.where(lane < 5120, near // 128, far % 256 // 32))
    slot = jnp.where(lane < 4096, lane % 512, jnp.where(lane < 5120, near % 128, far % 32))
    which = jnp.where(lane < 5120, plane, far // 256)
    spot = (slot + 128 * (head % 4)) % 512
    position = which * SPAN + block * 512 + row_of(spot, head >= 4)
    live = position < count
    bias = jnp.where(live, 0.0, DEAD)
    double = jnp.where((lane >= 5120) & (slot < 8), 1.0, 0.0)
    extra_row = lax.broadcasted_iota(jnp.int32, (32, LANES_ALL), 0)
    key_extra = jnp.where(extra_row == 0, bias, jnp.where(extra_row == 1, double, 0.0)).astype(BF)
    query_extra = jnp.where(
        extra_row == 0, 1.0, jnp.where(extra_row == 1, double, 0.0)
    ).astype(BF)[:, :LANES_QUERY]

    queries = all_t[0:48, :LANES_QUERY].astype(F32) * SCALE_TWO
    high = queries.astype(BF)
    query_a[0:48, :] = high
    query_a[48:96, :] = (queries - high.astype(F32)).astype(BF)
    query_a[96:128, :] = query_extra

    value_t[0:48, :] = all_t[96:144, :]
    value_t[48:64, :] = jnp.ones((16, LANES_ALL), BF)
    value_t[64:128, :] = jnp.zeros((64, LANES_ALL), BF)
    for g in range(6):
        lanes = slice(1024 * g, 1024 * g + 1024)
        keys = all_t[48:96, lanes]
        key_a[lanes, :] = jnp.concatenate([keys, keys, key_extra[:, lanes]], axis=0).T
        value_a[lanes, :] = value_t[:, lanes].T

    @pl.loop(0, BLOCKS)
    def _(i):
        key_from = pl.multiple_of(i // 4 * 1024, 1024)
        query_from = pl.multiple_of(i * BLOCK, BLOCK)
        score = dot(key_a[pl.ds(key_from, 1024), :], query_a[:, pl.ds(query_from, BLOCK)])
        peak = jnp.max(score, axis=0, keepdims=True)
        prob = jnp.exp2(score - peak).astype(BF)
        probs[i] = prob
        outs[:, pl.ds(query_from, BLOCK)] = dot(value_t[0:64, pl.ds(key_from, 1024)], prob)
        stats[:, pl.ds(query_from, BLOCK)] = jnp.broadcast_to(peak, (8, BLOCK))

    live_row = live.astype(F32)
    tile_lane = lax.broadcasted_iota(jnp.int32, (1, 128), 1)
    far_ratio = [jnp.zeros((1, 128), F32) for _ in range(2)]
    far_dot = [jnp.zeros((1, 128), F32) for _ in range(2)]
    zeros = jnp.zeros((64, 1), BF)

    def write_grad(first, width, dots, ratio):
        back = all_t[144:192, first : first + width].astype(F32) * ratio
        grad_a[0:48, first : first + width] = back.astype(BF)
        rest = -dots * ratio
        one = rest.astype(BF).astype(F32)
        two = (rest - one).astype(BF).astype(F32)
        three = rest - one - two
        row = lax.broadcasted_iota(jnp.int32, (16, width), 0)
        tail = jnp.where(row == 0, one, jnp.where(row == 1, two, jnp.where(row == 2, three, 0.0)))
        grad_a[48:64, first : first + width] = tail.astype(BF)

    def finish(first, width, total_out, live_part):
        den = total_out[48:49] + 1.0 - live_part
        inverse = 1.0 / den
        att = (total_out[0:48] * (inverse * live_part)).astype(BF)
        back = all_t[144:192, first : first + width].astype(F32)
        dots = jnp.sum(att.astype(F32) * back, axis=0, keepdims=True)
        return att, dots, inverse

    for s in range(HEADS):
        first = 512 * s
        near_from = 4096 + 128 * s
        out_a = outs[:, first : first + 128]
        out_b = outs[:, near_from : near_from + 128]
        out_c = spread_tiles(outs[:, 5120:5376], s)
        peak_a = stats[0:1, first : first + 128]
        peak_b = stats[0:1, near_from : near_from + 128]
        peak_c = spread_tiles(stats[:, 5120:5376], s)[0:1]
        inside = tile_lane < 32
        peak_c = jnp.where(inside, peak_c, 2.0 * DEAD)
        peak = jnp.maximum(jnp.maximum(peak_a, peak_b), peak_c)
        gain_a = jnp.exp2(peak_a - peak)
        gain_b = jnp.exp2(peak_b - peak)
        gain_c = jnp.where(inside, jnp.exp2(peak_c - peak), 0.0)
        total = out_a * gain_a + out_b * gain_b + out_c * gain_c
        att, dots, inverse = finish(first, 128, total, live_row[:, first : first + 128])
        att_ref[s, :, 0:128] = att
        write_grad(first, 128, dots, gain_a * inverse)
        write_grad(near_from, 128, dots, gain_b * inverse)
        shift = 32 * (s % 4)
        packed_ratio = jnp.broadcast_to(jnp.where(inside, gain_c * inverse, 0.0), (8, 128))
        packed_dot = jnp.broadcast_to(jnp.where(inside, dots, 0.0), (8, 128))
        if shift:
            packed_ratio = pltpu.roll(packed_ratio, shift, 1)
            packed_dot = pltpu.roll(packed_dot, shift, 1)
        far_ratio[s // 4] = far_ratio[s // 4] + packed_ratio[0:1]
        far_dot[s // 4] = far_dot[s // 4] + packed_dot[0:1]
        att, dots, inverse = finish(
            first + 128, 384, outs[:, first + 128 : first + 512], live_row[:, first + 128 : first + 512]
        )
        att_ref[s, :, 128:512] = att
        write_grad(first + 128, 384, dots, inverse)
    for t in range(2):
        write_grad(5120 + 128 * t, 128, far_dot[t], far_ratio[t])
    grad_a[64:128, :] = jnp.zeros((64, LANES_QUERY), BF)

    none = jnp.zeros((16, BLOCK), BF)

    @pl.loop(0, BLOCKS)
    def _(i):
        query_from = pl.multiple_of(i * BLOCK, BLOCK)
        lanes = pl.ds(query_from, BLOCK)
        gap = jnp.zeros((16, BLOCK), BF)
        wide = jnp.zeros((64, BLOCK), BF)
        top = jnp.concatenate([all_t[0:48, lanes], gap, wide], axis=0)
        low = jnp.concatenate([wide, grad_a[0:48, lanes], gap], axis=0)
        right[i, 0:BLOCK, :] = top.T
        right[i, BLOCK : 2 * BLOCK, :] = low.T

    sums[...] = jnp.zeros((LANES_ALL, 128), F32)

    @pl.loop(0, BLOCKS)
    def _(i):
        key_from = pl.multiple_of(i // 4 * 1024, 1024)
        query_from = pl.multiple_of(i * BLOCK, BLOCK)
        change = dot(value_a[pl.ds(key_from, 1024), :], grad_a[:, pl.ds(query_from, BLOCK)])
        prob = probs[i]
        slope = (prob.astype(F32) * change).astype(BF)
        outs[0:48, pl.ds(query_from, BLOCK)] = dot(all_t[48:96, pl.ds(key_from, 1024)], slope)
        both = jnp.concatenate([slope, prob], axis=1)
        sums[pl.ds(key_from, 1024), :] += dot(both, right[i])

    near_t = sums[4096:5120, :].T
    for s in range(HEADS):
        own_t = sums[512 * s : 512 * s + 512, :].T
        first = 512 * s
        extra = outs[0:48, 4096 + 128 * s : 4224 + 128 * s]
        third = jnp.where(tile_lane < 32, spread_tiles(outs[0:48, 5120:5376], s), 0.0)
        tile = outs[0:48, first : first + 128] + extra + third
        out_ref[s, 0:48, 0:128] = (tile * SCALE).astype(BF)
        out_ref[s, 0:48, 128:512] = (outs[0:48, first + 128 : first + 512] * SCALE).astype(BF)
        tile = own_t[:, 0:128] + near_t[:, 128 * s : 128 * s + 128]
        out_ref[s, 48:96, 0:128] = (tile[0:48] * SCALE).astype(BF)
        out_ref[s, 96:144, 0:128] = tile[64:112].astype(BF)
        out_ref[s, 48:96, 128:512] = (own_t[0:48, 128:512] * SCALE).astype(BF)
        out_ref[s, 96:144, 128:512] = own_t[64:112, 128:512].astype(BF)
    far_t = sums[5120:6144, :].T
    for z in range(PLANES):
        far_out_ref[z, 0:48, :] = (far_t[0:48, 256 * z : 256 * z + 256] * SCALE).astype(BF)
        far_out_ref[z, 48:96, :] = far_t[64:112, 256 * z : 256 * z + 256].astype(BF)


def return_kernel(
    att_ref,
    part_ref,
    far_ref,
    grad_ref,
    query_out,
    key_out,
    value_out,
    weight_out,
    send,
    land,
    far_land,
    send_sem,
    recv_sem,
    own_sem,
    far_send_sem,
    far_recv_sem,
    far_own_sem,
):
    plane, head = place()
    enter(plane, head)
    far_copies = []
    for step in range(1, PLANES):
        to = (plane + step) % PLANES
        copy = remote(
            far_ref.at[to],
            far_land.at[plane],
            far_send_sem.at[step],
            far_recv_sem.at[step],
            to * HEADS + head,
        )
        copy.start()
        far_copies.append(copy)
    own = pltpu.make_async_copy(far_ref.at[plane], far_land.at[plane], far_own_sem)
    own.start()
    far_copies.append(own)

    def launch(group, source, first, last, to_first, to_last):
        copies = []
        for step in range(1, HEADS):
            to = (head + step) % HEADS
            copy = remote(
                source.at[to, first:last],
                land.at[head, to_first:to_last],
                send_sem.at[group, step],
                recv_sem.at[group, step],
                plane * HEADS + to,
            )
            copy.start()
            copies.append(copy)
        own = pltpu.make_async_copy(
            source.at[head, first:last], land.at[head, to_first:to_last], own_sem.at[group]
        )
        own.start()
        copies.append(own)
        return copies

    first = launch(0, att_ref, 0, 48, 0, 48)
    second = launch(1, part_ref, 0, 48, 48, 96)
    for copy in far_copies:
        copy.wait()
    far = far_land[0].astype(F32)
    for z in range(1, PLANES):
        far = far + far_land[z].astype(F32)
    tile_lane = lax.broadcasted_iota(jnp.int32, (1, 128), 1)
    for s in range(HEADS):
        extra = jnp.where(tile_lane < 32, spread_tiles(far, s), 0.0)
        send[s, :, 0:128] = (part_ref[s, 48:144, 0:128].astype(F32) + extra).astype(BF)
        send[s, :, 128:512] = part_ref[s, 48:144, 128:512]
    third = launch(2, send, 0, 96, 96, 192)
    orders = (order_matrix(False), order_matrix(True))

    def collect(part, half):
        pieces = []
        for turn in range(4):
            rows = land[4 * half + turn, 48 * part : 48 * part + 48, :]
            if turn:
                cut = 512 - 128 * turn
                rows = jnp.concatenate([rows[:, cut:], rows[:, :cut]], axis=1)
            pieces.append(rows)
        return jnp.concatenate(pieces, axis=0)

    def give(part, target):
        for half in range(2):
            target[:, 192 * half : 192 * half + 192] = dot_nt(
                orders[half], collect(part, half)
            ).astype(BF)

    for copy in first:
        copy.wait()
    for half in range(2):
        att = dot_nt(collect(0, half), orders[half]).astype(BF)
        weight_out[192 * half : 192 * half + 192, :] = dot(att, grad_ref[...])
    for copy in second:
        copy.wait()
    give(1, query_out)
    for copy in third:
        copy.wait()
    give(2, key_out)
    give(3, value_out)


def vmem(count):
    return [pl.BlockSpec(memory_space=pltpu.VMEM)] * count


def local(tile_count, query_rows, key_rows, value_rows, out_grad, out_weight):
    sems = pltpu.SemaphoreType.DMA
    smem = pl.BlockSpec(memory_space=pltpu.SMEM)
    land, far = pl.pallas_call(
        spread_kernel,
        out_shape=(
            jax.ShapeDtypeStruct((HEADS, 192, ROWS), BF),
            jax.ShapeDtypeStruct((PLANES, 96, 256), BF),
        ),
        in_specs=[smem] + vmem(5),
        out_specs=tuple(vmem(2)),
        scratch_shapes=[
            pltpu.VMEM((HEADS, 192, ROWS), BF),
            pltpu.VMEM((96, 256), BF),
            sems((3, HEADS)),
            sems((3, HEADS)),
            sems((3,)),
            sems((PLANES,)),
            sems((PLANES,)),
            sems,
        ],
        compiler_params=pltpu.CompilerParams(
            collective_id=0, has_side_effects=True, vmem_limit_bytes=VMEM_LIMIT
        ),
        name="spread",
    )(tile_count, query_rows, key_rows, value_rows, out_grad, out_weight)
    att, part, far_part = pl.pallas_call(
        attend_kernel,
        out_shape=(
            jax.ShapeDtypeStruct((HEADS, 48, ROWS), BF),
            jax.ShapeDtypeStruct((HEADS, 144, ROWS), BF),
            jax.ShapeDtypeStruct((PLANES, 96, 256), BF),
        ),
        in_specs=[smem] + vmem(2),
        out_specs=tuple(vmem(3)),
        scratch_shapes=[
            pltpu.VMEM((192, LANES_ALL), BF),
            pltpu.VMEM((128, LANES_QUERY), BF),
            pltpu.VMEM((LANES_ALL, 128), BF),
            pltpu.VMEM((LANES_ALL, 128), BF),
            pltpu.VMEM((128, LANES_ALL), BF),
            pltpu.VMEM((8, LANES_QUERY), F32),
            pltpu.VMEM((64, LANES_QUERY), F32),
            pltpu.VMEM((BLOCKS, 1024, BLOCK), BF),
            pltpu.VMEM((128, LANES_QUERY), BF),
            pltpu.VMEM((BLOCKS, 2 * BLOCK, 128), BF),
            pltpu.VMEM((LANES_ALL, 128), F32),
        ],
        compiler_params=pltpu.CompilerParams(vmem_limit_bytes=VMEM_LIMIT),
        name="attend",
    )(tile_count, land, far)
    query_grad, key_grad, value_grad, weight_part = pl.pallas_call(
        return_kernel,
        out_shape=(
            jax.ShapeDtypeStruct((ROWS, WIDTH), BF),
            jax.ShapeDtypeStruct((ROWS, WIDTH), BF),
            jax.ShapeDtypeStruct((ROWS, WIDTH), BF),
            jax.ShapeDtypeStruct((WIDTH, DEPTH), F32),
        ),
        in_specs=vmem(4),
        out_specs=tuple(vmem(4)),
        scratch_shapes=[
            pltpu.VMEM((HEADS, 96, ROWS), BF),
            pltpu.VMEM((HEADS, 192, ROWS), BF),
            pltpu.VMEM((PLANES, 96, 256), BF),
            sems((3, HEADS)),
            sems((3, HEADS)),
            sems((3,)),
            sems((PLANES,)),
            sems((PLANES,)),
            sems,
        ],
        compiler_params=pltpu.CompilerParams(
            collective_id=1, has_side_effects=True, vmem_limit_bytes=VMEM_LIMIT
        ),
        name="give_back",
    )(att, part, far_part, out_grad)
    weight_grad = lax.psum(weight_part, ("slide", "seq")) * (65536.0**-0.5)
    return query_grad, key_grad, value_grad, weight_grad


def solution(mesh):
    rows = P(("slide", "seq"), None)
    return jax.shard_map(
        local,
        mesh=mesh,
        in_specs=(P("slide"), rows, rows, rows, rows, P()),
        out_specs=(rows, rows, rows, P()),
        check_vma=False,
    )
```

time: 662 us -> 262 us (0.40); the launches traced: 652 us -> 261 us
  local copies, waits for them, and re-layouts: 164 us -> 2.25 us
  Pallas kernels: 0 us -> 91 us
  matrix products: 83.6 us -> 0 us
  other arithmetic: 85.9 us -> 2.36 us
  starting transfers between devices: 78.8 us -> 0.04 us
  waiting for transfers between devices: 222 us -> 151 us
    pallas_call x0 -> x3, Pallas kernels: none -> 91 us  [the longest x1 39.8 us: local(): pl.pallas_call(attend_kernel, out_shape=(jax.ShapeDtypeStruct((HEADS, 48,...]
    dot_general x26 -> x0, matrix products: 83.6 us -> none  [the longest x4 17.7 us: one_block(): jnp.einsum('shqk,sqhd->skhd', prob_grid.astype(jnp.bfloat16), grad_blk, p...]
    ppermute x56 -> x0, starting transfers between devices: 78.7 us -> none  [from_partner(): lax.ppermute(value, axis, [(i, i ^ 1 << stride) for i in range(lax.axis_s...]
    ppermute x56 -> x0, waiting for transfers between devices: 66.9 us -> none  [from_partner(): lax.ppermute(value, axis, [(i, i ^ 1 << stride) for i in range(lax.axis_s...]
    broadcast_in_dim x71 -> x0, local copies, waits for them, and re-layouts: 58.1 us -> none  [reverse_dilation(): spread_rows = jnp.where(chosen_rows, value_matrix[:, None], filler_value)]
    another operation x34 -> x0, local copies, waits for them, and re-layouts: 51.1 us -> none  [the longest x24 47.8 us: apply_dilation(): value_matrix.reshape((value_matrix.shape[0] // dilation_rate, dilation_ra...]
    select_n x65 -> x0, other arithmetic: 43.2 us -> none  [the longest x36 28.6 us: doubling(): jnp.where(upper_half, jnp.concatenate([far_rows, near_rows], 0), jnp.conc...]
    gather x32 -> x0, local copies, waits for them, and re-layouts: 29.5 us -> none  [apply_dilation(): reshaped[:, np.arange(head_number) % dilation_rate, np.arange(head_number)]]
  transfers between devices with their start and end apart: 57 -> 1, of which waited for: 23 -> 1; matrix products, arithmetic and copies ran while one was open for 38% -> 0% of each run, Pallas kernels for 0% -> 0%
where the time goes in v1:
time: 262 us; the launch traced here: 261 us
  waiting for transfers between devices  151 us (58%)
  Pallas kernels  91 us (35%)
  between operations  14.7 us (6%)
    psum x1, waiting for transfers between devices, local(): weight_grad = lax.psum(weight_part, ('slide', 'seq')) * 65536.0 ** (-0.5)  151 us
    pallas_call x1, Pallas kernels, local(): pl.pallas_call(attend_kernel, out_shape=(jax.ShapeDtypeStruct((HEADS, 48,...  39.8 us
    pallas_call x1, Pallas kernels, local(): pl.pallas_call(spread_kernel, out_shape=(jax.ShapeDtypeStruct((HEADS, 192...  30.3 us
    pallas_call x1, Pallas kernels, local(): pl.pallas_call(return_kernel, out_shape=(jax.ShapeDtypeStruct((ROWS, WIDT...  20.9 us
  transfers between devices with their start and end apart: 1, of which 1 were waited for; matrix products, arithmetic and copies ran while one was open for 0% of the time, Pallas kernels for 0%

profile of v1, /device:TPU:1, one launch (start us, length us, event | category | flops | bytes accessed | tf_op | source)
XLA Modules:
  0.0 261.3 jit_solution(11524506225679144995)
XLA Ops:
  7.2 0.0 all-reduce.2.cloned.1.call-start
  7.9 30.3 %spread.1 = (bf16[8,192,512]{2,1,0:T(8,128)(2,1)}, bf16[4,96,256]{2,1,0:T(8,128)(2,1)}) custom-call(s32[1]{0:T(128)S(6)} %copy.14.count_ref, bf16[512,384]{1,0:T(8,128)(2,1)} %query_ref.1, bf16[512,384]{1,0:T(8,128)(2,1)} %key_ref.1, bf16[512,384]{1,0:T(8,128)(2,1)} %value_ref.1, bf16[512,768]{1,0:T(8,128)(2,1)} %grad_ref.3, bf16[384,768]{1,0:T(8,128)(2,1)} %weight_ref.1), custom_call_target="tpu_custom_call" | custom-call | tf_op jit(solution)/shard_map/spread/pallas_call | solution.py:462
  38.1 39.8 %attend.1 = (bf16[8,48,512]{2,1,0:T(8,128)(2,1)}, bf16[8,144,512]{2,1,0:T(8,128)(2,1)}, bf16[4,96,256]{2,1,0:T(8,128)(2,1)}) custom-call(s32[1]{0:T(128)S(6)} %copy.14.count_ref, bf16[8,192,512]{2,1,0:T(8,128)(2,1)} %get-tuple-element.13.land_ref, bf16[4,96,256]{2,1,0:T(8,128)(2,1)} %get-tuple-element.14.far_ref), custom_call_target="tpu_custom_call" | custom-call | tf_op jit(solution)/shard_map/attend/pallas_call | solution.py:485
  77.9 20.9 %give_back.1 = (bf16[512,384]{1,0:T(8,128)(2,1)}, bf16[512,384]{1,0:T(8,128)(2,1)}, bf16[512,384]{1,0:T(8,128)(2,1)}, f32[384,768]{1,0:T(8,128)}) custom-call(bf16[8,48,512]{2,1,0:T(8,128)(2,1)} %get-tuple-element.15.att_ref, bf16[8,144,512]{2,1,0:T(8,128)(2,1)} %get-tuple-element.16.part_ref, bf16[4,96,256]{2,1,0:T(8,128)(2,1)} %get-tuple-element.17.far_ref, ...), custom_call_target="tpu_custom_call" | custom-call | tf_op jit(solution)/shard_map/give_back/pallas_call | solution.py:510
  98.8 0.0 all-reduce.2.cloned.1.call-update
  98.9 0.0 copy-start.2
  98.9 0.0 copy-start.1
  98.9 150.9 %all-reduce.2.cloned.1.call-done = f32[384,768]{1,0:T(8,128)} async-done(((f32[384,768]{1,0:T(8,128)}), f32[384,768]{1,0:T(8,128)}) %all-reduce.2.cloned.1.call-update) | async-done | bytes 1179664 | tf_op jit(solution)/shard_map/psum | solution.py:536
  249.8 2.4 broadcast_multiply_fusion
  252.2 0.0 copy-done.2
  252.2 0.0 copy-start
  252.2 0.7 copy.15
  252.9 0.0 copy-done.1
  252.9 0.7 copy.16
  253.7 0.0 copy-done
  253.7 0.7 copy.17
Async XLA Ops:
  7.2 242.7 %all-reduce.2.cloned.1.call-start = ((), (), s32[]{:S(2)}) async-start(), calls=%async_computation | async-start | bytes 2359296 | tf_op jit(solution)/shard_map/psum | solution.py:536
  98.9 153.3 %copy-start.2 = (bf16[512,384]{1,0:T(8,128)(2,1)S(1)}, bf16[512,384]{1,0:T(8,128)(2,1)}, u32[]{:S(2)}) copy-start(bf16[512,384]{1,0:T(8,128)(2,1)} %get-tuple-element.26) | copy-start | bytes 1179652
  98.9 154.1 %copy-start.1 = (bf16[512,384]{1,0:T(8,128)(2,1)S(1)}, bf16[512,384]{1,0:T(8,128)(2,1)}, u32[]{:S(2)}) copy-start(bf16[512,384]{1,0:T(8,128)(2,1)} %get-tuple-element.27) | copy-start | bytes 1179652
  252.2 1.5 copy-start
Sparse Core Ops, SparseCore 0:
  99.0 150.7 all-reduce.1

commit v2 on v1

v2 whole, which is shorter than its diff:
```python
import jax
import jax.numpy as jnp
from jax import lax
from jax.experimental import pallas as pl
from jax.experimental.pallas import tpu as pltpu
from jax.sharding import PartitionSpec as P

HEAD_WIDTH = 48
HEADS = 8
ROWS = 512
SPAN = 4096
WIDTH = 384
DEPTH = 768
PLANES = 4
LANES_ALL = 6144
LANES_QUERY = 5376
BLOCK = 256
BLOCKS = LANES_QUERY // BLOCK
DEAD = -1e30
SCALE = float(HEAD_WIDTH) ** -0.5
SCALE_TWO = SCALE * 1.4426950408889634
BF = jnp.bfloat16
F32 = jnp.float32
VMEM_LIMIT = 56 * 1024 * 1024


def dot(lhs, rhs):
    return jnp.dot(lhs, rhs, preferred_element_type=F32)


def dot_nt(lhs, rhs):
    return lax.dot_general(lhs, rhs, (((1,), (1,)), ((), ())), preferred_element_type=F32)


def row_of(slot, swap):
    a, b, c, d = slot // 128, slot // 32 % 4, slot // 8 % 4, slot % 8
    b = jnp.where(b < 2, jnp.where(swap, 1 - b, b), b)
    return a + 4 * b + 16 * c + 64 * d


def order_matrix(swap):
    rows = lax.broadcasted_iota(jnp.int32, (ROWS, ROWS), 0)
    slots = lax.broadcasted_iota(jnp.int32, (ROWS, ROWS), 1)
    return jnp.where(rows == row_of(slots, swap), 1.0, 0.0).astype(BF)


def place():
    seq = lax.axis_index("seq")
    return seq // HEADS, seq % HEADS


def spread_tiles(value, s):
    tile = value[:, 128 * (s // 4) : 128 * (s // 4) + 128]
    shift = (128 - 32 * (s % 4)) % 128
    return pltpu.roll(tile, shift, 1) if shift else tile


MESH = pl.DeviceIdType.MESH


def fused_kernel(
    count_ref,
    query_ref,
    key_ref,
    value_ref,
    grad_ref,
    weight_ref,
    query_out,
    key_out,
    value_out,
    weight_out,
    send,
    all_t,
    far_send,
    far_land,
    query_a,
    key_a,
    value_a,
    value_t,
    stats,
    outs,
    probs,
    grad_a,
    right,
    sums,
    att_send,
    far_part,
    far_back,
    far_wide,
    give,
    land,
    first_send,
    first_land,
    plane_part,
    plane_land,
    slide_part,
    slide_land,
    last_part,
    last_land,
    order_a,
    order_b,
    send_sem,
    recv_sem,
    own_sem,
):
    plane, head = place()
    slide = lax.axis_index("slide")
    count = count_ref[0]
    orders = (order_a, order_b)
    order_a[...] = order_matrix(False)
    order_b[...] = order_matrix(True)
    plane_peers = [(plane * HEADS + (head + t) % HEADS, (head + t) % HEADS) for t in range(1, HEADS)]
    far_peers = [((plane + t) % PLANES * HEADS + head, (plane + t) % PLANES) for t in range(1, PLANES)]
    slide_peers = [(slide + t) % PLANES for t in range(1, PLANES)]

    def remote(stage, source, target, axis, peer, mine, theirs):
        send_copy = pltpu.make_async_remote_copy(
            src_ref=source,
            dst_ref=target,
            send_sem=send_sem.at[stage, theirs],
            recv_sem=recv_sem.at[stage, mine],
            device_id={axis: peer},
            device_id_type=MESH,
        )
        send_copy.start()
        wait_copy = pltpu.make_async_remote_copy(
            src_ref=source,
            dst_ref=target,
            send_sem=send_sem.at[stage, theirs],
            recv_sem=recv_sem.at[stage, theirs],
            device_id={axis: peer},
            device_id_type=MESH,
        )
        return wait_copy

    def own_copy(stage, source, target):
        copy = pltpu.make_async_copy(source, target, own_sem.at[stage])
        copy.start()
        return copy

    def wait_all(copies):
        for copy in copies:
            copy.wait()

    def stage_in(part, value_t):
        for half in range(2):
            moved = dot(value_t[192 * half : 192 * half + 192], orders[half][...]).astype(BF)
            for turn in range(4):
                rows = moved[48 * turn : 48 * turn + 48]
                if turn:
                    rows = jnp.concatenate([rows[:, 128 * turn :], rows[:, : 128 * turn]], axis=1)
                send[4 * half + turn, 48 * part : 48 * part + 48, :] = rows

    my_lanes = pl.ds(pl.multiple_of(head * 512, 512), 512)

    def launch(stage, first, last):
        copies = [
            remote(stage, send.at[to, first:last], all_t.at[first:last, my_lanes], "seq", peer, head, to)
            for peer, to in plane_peers
        ]
        return copies + [own_copy(stage, send.at[head, first:last], all_t.at[first:last, my_lanes])]

    stage_in(1, key_ref[...].T)
    stage_in(0, query_ref[...].T)
    barrier = pltpu.get_barrier_semaphore()
    for peer, _ in plane_peers + far_peers:
        pl.semaphore_signal(barrier, inc=1, device_id={"seq": peer}, device_id_type=MESH)
    for peer in slide_peers:
        pl.semaphore_signal(barrier, inc=1, device_id={"slide": peer}, device_id_type=MESH)
    pl.semaphore_wait(barrier, 13)
    first = launch(0, 0, 96)
    stage_in(2, value_ref[...].T)
    second = launch(1, 96, 144)
    lane = lax.broadcasted_iota(jnp.int32, (1, ROWS), 1)
    own_live = (plane * SPAN + head * ROWS + lane < count).astype(F32)
    back = (dot_nt(weight_ref[...], grad_ref[...]) * own_live).astype(BF)
    stage_in(3, back)
    third = launch(2, 144, 192)

    lane = lax.broadcasted_iota(jnp.int32, (1, LANES_ALL), 1)
    near = lane - 4096
    far = lane - 5120
    block = jnp.where(lane < 4096, lane // 512, jnp.where(lane < 5120, near // 128, far % 256 // 32))
    slot = jnp.where(lane < 4096, lane % 512, jnp.where(lane < 5120, near % 128, far % 32))
    which = jnp.where(lane < 5120, plane, far // 256)
    spot = (slot + 128 * (head % 4)) % 512
    position = which * SPAN + block * 512 + row_of(spot, head >= 4)
    live = position < count
    bias = jnp.where(live, 0.0, DEAD)
    double = jnp.where((lane >= 5120) & (slot < 8), 1.0, 0.0)
    extra_row = lax.broadcasted_iota(jnp.int32, (32, LANES_ALL), 0)
    key_extra = jnp.where(extra_row == 0, bias, jnp.where(extra_row == 1, double, 0.0)).astype(BF)
    query_extra = jnp.where(
        extra_row == 0, 1.0, jnp.where(extra_row == 1, double, 0.0)
    ).astype(BF)[:, :LANES_QUERY]
    query_a[96:128, :] = query_extra
    value_t[48:64, :] = jnp.ones((16, LANES_ALL), BF)
    value_t[64:128, :] = jnp.zeros((64, LANES_ALL), BF)
    here = lax.broadcasted_iota(jnp.int32, (1024, 256), 0)
    there = lax.broadcasted_iota(jnp.int32, (1024, 256), 1)
    pick = jnp.where(here == there // 32 * 128 + there % 32, 1.0, 0.0).astype(BF)

    def near_tiles(first, last):
        for s in range(HEADS):
            all_t[first:last, 4096 + 128 * s : 4224 + 128 * s] = all_t[first:last, 512 * s : 512 * s + 128]

    def build_query(first, last):
        queries = all_t[0:48, first:last].astype(F32) * SCALE_TWO
        high = queries.astype(BF)
        query_a[0:48, first:last] = high
        query_a[48:96, first:last] = (queries - high.astype(F32)).astype(BF)

    def build_key(g):
        lanes = slice(1024 * g, 1024 * g + 1024)
        keys = all_t[48:96, lanes]
        key_a[lanes, :] = jnp.concatenate([keys, keys, key_extra[:, lanes]], axis=0).T

    def build_value(g):
        lanes = slice(1024 * g, 1024 * g + 1024)
        value_t[0:48, lanes] = all_t[96:144, lanes]
        value_a[lanes, :] = value_t[:, lanes].T

    wait_all(first)
    near_tiles(0, 96)
    all_t[0:48, 5120:5376] = dot(all_t[0:48, 4096:5120], pick).astype(BF)
    build_query(0, LANES_QUERY)
    for g in range(5):
        build_key(g)
    wait_all(second)
    near_tiles(96, 144)
    far_send[...] = dot(all_t[48:144, 4096:5120], pick).astype(BF)
    fourth = [
        remote(3, far_send, far_land.at[plane], "seq", peer, plane, to) for peer, to in far_peers
    ] + [own_copy(3, far_send, far_land.at[plane])]
    for g in range(5):
        build_value(g)

    def forward(i):
        key_from = pl.multiple_of(i // 4 * 1024, 1024)
        query_from = pl.multiple_of(i * BLOCK, BLOCK)
        score = dot(key_a[pl.ds(key_from, 1024), :], query_a[:, pl.ds(query_from, BLOCK)])
        peak = jnp.max(score, axis=0, keepdims=True)
        prob = jnp.exp2(score - peak).astype(BF)
        probs[i] = prob
        outs[:, pl.ds(query_from, BLOCK)] = dot(value_t[0:64, pl.ds(key_from, 1024)], prob)
        stats[:, pl.ds(query_from, BLOCK)] = jnp.broadcast_to(peak, (8, BLOCK))

    @pl.loop(0, BLOCKS - 1)
    def _(i):
        forward(i)

    wait_all(fourth)
    for z in range(PLANES):
        all_t[48:144, 5120 + 256 * z : 5376 + 256 * z] = far_land[z]
    build_key(5)
    build_value(5)
    forward(BLOCKS - 1)
    wait_all(third)
    near_tiles(144, 192)
    all_t[144:192, 5120:5376] = dot(all_t[144:192, 4096:5120], pick).astype(BF)
    live_row = live.astype(F32)
    tile_lane = lax.broadcasted_iota(jnp.int32, (1, 128), 1)
    inside = tile_lane < 32
    far_ratio = [jnp.zeros((1, 128), F32) for _ in range(2)]
    far_dot = [jnp.zeros((1, 128), F32) for _ in range(2)]

    def write_grad(first, width, dots, ratio):
        back = all_t[144:192, first : first + width].astype(F32) * ratio
        grad_a[0:48, first : first + width] = back.astype(BF)
        rest = -dots * ratio
        one = rest.astype(BF).astype(F32)
        two = (rest - one).astype(BF).astype(F32)
        three = rest - one - two
        row = lax.broadcasted_iota(jnp.int32, (16, width), 0)
        tail = jnp.where(row == 0, one, jnp.where(row == 1, two, jnp.where(row == 2, three, 0.0)))
        grad_a[48:64, first : first + width] = tail.astype(BF)

    def finish(first, width, total_out, live_part):
        den = total_out[48:49] + 1.0 - live_part
        inverse = 1.0 / den
        att = (total_out[0:48] * (inverse * live_part)).astype(BF)
        back = all_t[144:192, first : first + width].astype(F32)
        dots = jnp.sum(att.astype(F32) * back, axis=0, keepdims=True)
        return att, dots, inverse

    for s in range(HEADS):
        first = 512 * s
        near_from = 4096 + 128 * s
        out_a = outs[:, first : first + 128]
        out_b = outs[:, near_from : near_from + 128]
        out_c = spread_tiles(outs[:, 5120:5376], s)
        peak_a = stats[0:1, first : first + 128]
        peak_b = stats[0:1, near_from : near_from + 128]
        peak_c = spread_tiles(stats[:, 5120:5376], s)[0:1]
        peak_c = jnp.where(inside, peak_c, 2.0 * DEAD)
        peak = jnp.maximum(jnp.maximum(peak_a, peak_b), peak_c)
        gain_a = jnp.exp2(peak_a - peak)
        gain_b = jnp.exp2(peak_b - peak)
        gain_c = jnp.where(inside, jnp.exp2(peak_c - peak), 0.0)
        total = out_a * gain_a + out_b * gain_b + out_c * gain_c
        att, dots, inverse = finish(first, 128, total, live_row[:, first : first + 128])
        att_send[s, :, 0:128] = att
        write_grad(first, 128, dots, gain_a * inverse)
        write_grad(near_from, 128, dots, gain_b * inverse)
        shift = 32 * (s % 4)
        packed_ratio = jnp.broadcast_to(jnp.where(inside, gain_c * inverse, 0.0), (8, 128))
        packed_dot = jnp.broadcast_to(jnp.where(inside, dots, 0.0), (8, 128))
        if shift:
            packed_ratio = pltpu.roll(packed_ratio, shift, 1)
            packed_dot = pltpu.roll(packed_dot, shift, 1)
        far_ratio[s // 4] = far_ratio[s // 4] + packed_ratio[0:1]
        far_dot[s // 4] = far_dot[s // 4] + packed_dot[0:1]
        att, dots, inverse = finish(
            first + 128, 384, outs[:, first + 128 : first + 512], live_row[:, first + 128 : first + 512]
        )
        att_send[s, :, 128:512] = att
        write_grad(first + 128, 384, dots, inverse)
    for t in range(2):
        write_grad(5120 + 128 * t, 128, far_dot[t], far_ratio[t])
    grad_a[64:128, :] = jnp.zeros((64, LANES_QUERY), BF)
    fifth = [
        remote(4, att_send.at[to], land.at[head, 0:48], "seq", peer, head, to) for peer, to in plane_peers
    ] + [own_copy(4, att_send.at[head], land.at[head, 0:48])]

    @pl.loop(0, BLOCKS)
    def _(i):
        query_from = pl.multiple_of(i * BLOCK, BLOCK)
        lanes = pl.ds(query_from, BLOCK)
        gap = jnp.zeros((16, BLOCK), BF)
        wide = jnp.zeros((64, BLOCK), BF)
        top = jnp.concatenate([all_t[0:48, lanes], gap, wide], axis=0)
        low = jnp.concatenate([wide, grad_a[0:48, lanes], gap], axis=0)
        right[i, 0:BLOCK, :] = top.T
        right[i, BLOCK : 2 * BLOCK, :] = low.T

    sums[...] = jnp.zeros((LANES_ALL, 128), F32)

    def backward(i):
        key_from = pl.multiple_of(i // 4 * 1024, 1024)
        query_from = pl.multiple_of(i * BLOCK, BLOCK)
        change = dot(value_a[pl.ds(key_from, 1024), :], grad_a[:, pl.ds(query_from, BLOCK)])
        prob = probs[i]
        slope = (prob.astype(F32) * change).astype(BF)
        outs[0:48, pl.ds(query_from, BLOCK)] = dot(all_t[48:96, pl.ds(key_from, 1024)], slope)
        both = jnp.concatenate([slope, prob], axis=1)
        sums[pl.ds(key_from, 1024), :] += dot(both, right[i])

    def backward_part(g):
        @pl.loop(0, 4)
        def _(i):
            backward(4 * g + i)

    backward(BLOCKS - 1)
    far_t = sums[5120:6144, :].T
    for z in range(PLANES):
        far_part[z, 0:48, :] = far_t[0:48, 256 * z : 256 * z + 256].astype(BF)
        far_part[z, 48:96, :] = far_t[64:112, 256 * z : 256 * z + 256].astype(BF)
    sixth = [
        remote(5, far_part.at[to], far_back.at[plane], "seq", peer, plane, to) for peer, to in far_peers
    ] + [own_copy(5, far_part.at[plane], far_back.at[plane])]
    backward_part(4)

    def collect(part, half):
        pieces = []
        for turn in range(4):
            rows = land[4 * half + turn, 48 * part : 48 * part + 48, :]
            if turn:
                cut = 512 - 128 * turn
                rows = jnp.concatenate([rows[:, cut:], rows[:, :cut]], axis=1)
            pieces.append(rows)
        return jnp.concatenate(pieces, axis=0)

    wait_all(fifth)
    for half in range(2):
        att = dot_nt(collect(0, half), orders[half][...]).astype(BF)
        part = dot(att, grad_ref[...]).astype(BF)
        for turn in range(4):
            first_send[4 * half + turn] = part[48 * turn : 48 * turn + 48]
    seventh = [
        remote(6, first_send.at[to], first_land.at[head], "seq", peer, head, to) for peer, to in plane_peers
    ] + [own_copy(6, first_send.at[head], first_land.at[head])]

    wait_all(sixth)
    far_sum = far_back[0].astype(F32)
    for z in range(1, PLANES):
        far_sum = far_sum + far_back[z].astype(F32)
    for s in range(HEADS):
        lanes = slice(128 * s, 128 * s + 128)
        far_wide[0:48, lanes] = jnp.where(inside, spread_tiles(outs[0:48, 5120:5376], s), 0.0)
        far_wide[48:144, lanes] = jnp.where(inside, spread_tiles(far_sum, s), 0.0)

    def total(ref):
        value = ref[0].astype(F32)
        for t in range(1, ref.shape[0]):
            value = value + ref[t].astype(F32)
        return value

    returned = []
    for turn in range(1, 5):
        g = (head // 2 + turn) % 4
        backward_part(g)
        for e in range(2):
            s = 2 * g + e
            lanes = pl.ds(pl.multiple_of(128 * s, 128), 128)
            near_lanes = pl.ds(pl.multiple_of(4096 + 128 * s, 128), 128)
            own_t = sums[pl.ds(pl.multiple_of(512 * s, 512), 512), :].T
            near_t = sums[near_lanes, :].T
            mine = outs[0:48, pl.ds(pl.multiple_of(512 * s, 512), 512)]
            tile = mine[:, 0:128] + outs[0:48, near_lanes] + far_wide[0:48, lanes]
            give[s, 0:48, 0:128] = (tile * SCALE).astype(BF)
            give[s, 0:48, 128:512] = (mine[:, 128:512] * SCALE).astype(BF)
            tile = own_t[0:48, 0:128] + near_t[0:48] + far_wide[48:96, lanes]
            give[s, 48:96, 0:128] = (tile * SCALE).astype(BF)
            give[s, 48:96, 128:512] = (own_t[0:48, 128:512] * SCALE).astype(BF)
            tile = own_t[64:112, 0:128] + near_t[64:112] + far_wide[96:144, lanes]
            give[s, 96:144, 0:128] = tile.astype(BF)
            give[s, 96:144, 128:512] = own_t[64:112, 128:512].astype(BF)
            target = land.at[head, 48:192]
            if turn < 4:
                returned.append(remote(7, give.at[s], target, "seq", plane * HEADS + s, head, s))
        if turn == 4:
            other = head + 1 - 2 * (head % 2)
            returned.append(
                remote(7, give.at[other], target, "seq", plane * HEADS + other, head, other)
            )
            returned.append(own_copy(7, give.at[head], target))
        if turn == 1:
            wait_all(seventh)
            plane_part[...] = total(first_land).astype(BF)
            eighth = [
                remote(8, plane_part, plane_land.at[plane], "seq", peer, plane, to)
                for peer, to in far_peers
            ] + [own_copy(8, plane_part, plane_land.at[plane])]
        if turn == 2:
            wait_all(eighth)
            slide_part[...] = total(plane_land).astype(BF)
            ninth = [
                remote(9, slide_part, slide_land.at[slide], "slide", peer, slide, peer)
                for peer in slide_peers
            ] + [own_copy(9, slide_part, slide_land.at[slide])]
        if turn == 3:
            wait_all(ninth)
            last_part[...] = (total(slide_land) * (65536.0**-0.5)).astype(BF)
            tenth = [
                remote(10, last_part, last_land.at[head], "seq", peer, head, to)
                for peer, to in plane_peers
            ] + [own_copy(10, last_part, last_land.at[head])]
    wait_all(tenth)
    for h in range(HEADS):
        weight_out[48 * h : 48 * h + 48, :] = last_land[h].astype(F32)
    wait_all(returned)
    for part, target in ((1, query_out), (2, key_out), (3, value_out)):
        for half in range(2):
            target[:, 192 * half : 192 * half + 192] = dot_nt(
                orders[half][...], collect(part, half)
            ).astype(BF)


def vmem(count):
    return [pl.BlockSpec(memory_space=pltpu.VMEM)] * count


def local(tile_count, query_rows, key_rows, value_rows, out_grad, out_weight):
    sems = pltpu.SemaphoreType.DMA
    smem = pl.BlockSpec(memory_space=pltpu.SMEM)
    return pl.pallas_call(
        fused_kernel,
        out_shape=(
            jax.ShapeDtypeStruct((ROWS, WIDTH), BF),
            jax.ShapeDtypeStruct((ROWS, WIDTH), BF),
            jax.ShapeDtypeStruct((ROWS, WIDTH), BF),
            jax.ShapeDtypeStruct((WIDTH, DEPTH), F32),
        ),
        in_specs=[smem] + vmem(5),
        out_specs=tuple(vmem(4)),
        scratch_shapes=[
            pltpu.VMEM((HEADS, 192, ROWS), BF),
            pltpu.VMEM((192, LANES_ALL), BF),
            pltpu.VMEM((96, 256), BF),
            pltpu.VMEM((PLANES, 96, 256), BF),
            pltpu.VMEM((128, LANES_QUERY), BF),
            pltpu.VMEM((LANES_ALL, 128), BF),
            pltpu.VMEM((LANES_ALL, 128), BF),
            pltpu.VMEM((128, LANES_ALL), BF),
            pltpu.VMEM((8, LANES_QUERY), F32),
            pltpu.VMEM((64, LANES_QUERY), F32),
            pltpu.VMEM((BLOCKS, 1024, BLOCK), BF),
            pltpu.VMEM((128, LANES_QUERY), BF),
            pltpu.VMEM((BLOCKS, 2 * BLOCK, 128), BF),
            pltpu.VMEM((LANES_ALL, 128), F32),
            pltpu.VMEM((HEADS, 48, ROWS), BF),
            pltpu.VMEM((PLANES, 96, 256), BF),
            pltpu.VMEM((PLANES, 96, 256), BF),
            pltpu.VMEM((144, 1024), F32),
            pltpu.VMEM((HEADS, 144, ROWS), BF),
            pltpu.VMEM((HEADS, 192, ROWS), BF),
            pltpu.VMEM((HEADS, 48, DEPTH), BF),
            pltpu.VMEM((HEADS, 48, DEPTH), BF),
            pltpu.VMEM((48, DEPTH), BF),
            pltpu.VMEM((PLANES, 48, DEPTH), BF),
            pltpu.VMEM((48, DEPTH), BF),
            pltpu.VMEM((PLANES, 48, DEPTH), BF),
            pltpu.VMEM((48, DEPTH), BF),
            pltpu.VMEM((HEADS, 48, DEPTH), BF),
            pltpu.VMEM((ROWS, ROWS), BF),
            pltpu.VMEM((ROWS, ROWS), BF),
            sems((11, HEADS)),
            sems((11, HEADS)),
            sems((11,)),
        ],
        compiler_params=pltpu.CompilerParams(
            collective_id=0, has_side_effects=True, vmem_limit_bytes=VMEM_LIMIT
        ),
        name="layer_back",
    )(tile_count, query_rows, key_rows, value_rows, out_grad, out_weight)


def solution(mesh):
    rows = P(("slide", "seq"), None)
    return jax.shard_map(
        local,
        mesh=mesh,
        in_specs=(P("slide"), rows, rows, rows, rows, P()),
        out_specs=(rows, rows, rows, P()),
        check_vma=False,
    )
```

time: 262 us -> 99 us (0.38)
  waiting for transfers between devices: 151 us -> 0 us
  between operations: 14.7 us -> 1.3 us
  local copies, waits for them, and re-layouts: 2.25 us -> 5.44 us
    psum x1 -> x0, waiting for transfers between devices: 151 us -> none  [local(): weight_grad = lax.psum(weight_part, ('slide', 'seq')) * 65536.0 ** (-0.5)]
    unnamed x9 -> x8, local copies, waits for them, and re-layouts: 2.25 us -> 5.44 us
    pallas_call x3 -> x1, Pallas kernels: 91 us -> 90.6 us  [local(): pl.pallas_call(fused_kernel, out_shape=(jax.ShapeDtypeStruct((ROWS, WIDTH...]
  transfers between devices with their start and end apart: 1 -> 0, of which waited for: 1 -> 0; matrix products, arithmetic and copies ran while one was open for 0% -> 0% of each run, Pallas kernels for 0% -> 0%
where the time goes in v2:
time: 99 us; the launch traced here: 97.3 us
  Pallas kernels  90.6 us (92%)
  local copies, waits for them, and re-layouts  5.44 us (5%)
  between operations  1.3 us (1%)
    pallas_call x1, Pallas kernels, local(): pl.pallas_call(fused_kernel, out_shape=(jax.ShapeDtypeStruct((ROWS, WIDTH...  90.6 us
    unnamed x8, local copies, waits for them, and re-layouts  5.44 us

profile of v2, /device:TPU:1, one launch (start us, length us, event | category | flops | bytes accessed | tf_op | source)
XLA Modules:
  0.0 97.3 jit_solution(4485782980754910973)
XLA Ops:
  1.3 90.6 %layer_back.1 = (bf16[512,384]{1,0:T(8,128)(2,1)}, bf16[512,384]{1,0:T(8,128)(2,1)}, bf16[512,384]{1,0:T(8,128)(2,1)}, f32[384,768]{1,0:T(8,128)}) custom-call(s32[1]{0:T(128)S(6)} %copy.14.count_ref, bf16[512,384]{1,0:T(8,128)(2,1)} %query_ref.1, bf16[512,384]{1,0:T(8,128)(2,1)} %key_ref.1, bf16[512,384]{1,0:T(8,128)(2,1)} %value_ref.1, ...), custom_call_target="tpu_custom_call" | custom-call | tf_op jit(solution)/shard_map/layer_back/pallas_call | solution.py:466
  91.9 0.0 copy-start.1
  91.9 0.0 copy-start
  91.9 1.9 %copy.15 = bf16[512,384]{1,0:T(8,128)(2,1)} copy(bf16[512,384]{1,0:T(8,128)(2,1)} %get-tuple-element.8) | data formatting | bytes 786432
  93.8 1.8 %copy.16 = bf16[512,384]{1,0:T(8,128)(2,1)} copy(bf16[512,384]{1,0:T(8,128)(2,1)} %get-tuple-element.9) | data formatting | bytes 786432
  95.6 0.0 copy-done.1
  95.6 0.7 copy.17
  96.3 0.0 copy-done
  96.3 1.0 %copy.18 = f32[384,768]{1,0:T(8,128)} copy(f32[384,768]{1,0:T(8,128)S(1)} %copy-done) | data formatting | bytes 2359296
Async XLA Ops:
  91.9 3.7 %copy-start.1 = (bf16[512,384]{1,0:T(8,128)(2,1)S(1)}, bf16[512,384]{1,0:T(8,128)(2,1)}, u32[]{:S(2)}) copy-start(bf16[512,384]{1,0:T(8,128)(2,1)} %get-tuple-element.10) | copy-start | bytes 1179652
  91.9 4.4 %copy-start = (f32[384,768]{1,0:T(8,128)S(1)}, f32[384,768]{1,0:T(8,128)}, u32[]{:S(2)}) copy-start(f32[384,768]{1,0:T(8,128)} %get-tuple-element.11) | copy-start | bytes 3538948

commit v3 on v2

--- a/solution.py
+++ b/solution.py
@@ -16,6 +16,7 @@
 LANES_QUERY = 5376
 BLOCK = 256
 BLOCKS = LANES_QUERY // BLOCK
+CHUNK = 256
 DEAD = -1e30
 SCALE = float(HEAD_WIDTH) ** -0.5
 SCALE_TWO = SCALE * 1.4426950408889634
@@ -56,6 +57,7 @@
 
 
 MESH = pl.DeviceIdType.MESH
+POINTS = (1, 3, 5, 7, 9)
 
 
 def fused_kernel(
@@ -89,14 +91,21 @@
     far_wide,
     give,
     land,
-    first_send,
-    first_land,
-    plane_part,
-    plane_land,
-    slide_part,
-    slide_land,
+    core_send,
+    core_land,
+    far_first,
+    far_second,
+    ring_part,
+    ring_land,
+    cross_part,
+    cross_land,
     last_part,
     last_land,
+    final_land,
+    score_a,
+    score_b,
+    top_a,
+    top_b,
     order_a,
     order_b,
     send_sem,
@@ -106,20 +115,38 @@
     plane, head = place()
     slide = lax.axis_index("slide")
     count = count_ref[0]
+    core = slide % 2
+    across = slide // 2
+    tall, flat = head // 4, head % 4
+    barrier = pltpu.get_barrier_semaphore()
     orders = (order_a, order_b)
+    plane_peers = [(plane * HEADS + (head + t) % HEADS, (head + t) % HEADS) for t in range(1, HEADS)]
+    far_peers = [((plane + t) % PLANES * HEADS + head, (plane + t) % PLANES) for t in range(1, PLANES)]
+    ring_peers = [
+        (plane * HEADS + tall * 4 + (flat + t) % 4, (flat + t) % 4) for t in range(1, PLANES)
+    ]
+    other_core = slide + 1 - 2 * core
+    cross_peers = []
+    for step_across, step_tall in ((0, 1), (1, 0), (1, 1)):
+        to_across = across + step_across * (1 - 2 * across)
+        to_tall = tall + step_tall * (1 - 2 * tall)
+        where = {"slide": to_across * 2 + core, "seq": plane * HEADS + to_tall * 4 + flat}
+        cross_peers.append((where, to_across * 2 + to_tall))
+    for peer, _ in plane_peers + far_peers:
+        pl.semaphore_signal(barrier, inc=1, device_id={"seq": peer}, device_id_type=MESH)
+    pl.semaphore_signal(barrier, inc=1, device_id={"slide": other_core}, device_id_type=MESH)
+    for where, _ in cross_peers[1:]:
+        pl.semaphore_signal(barrier, inc=1, device_id=where, device_id_type=MESH)
     order_a[...] = order_matrix(False)
     order_b[...] = order_matrix(True)
-    plane_peers = [(plane * HEADS + (head + t) % HEADS, (head + t) % HEADS) for t in range(1, HEADS)]
-    far_peers = [((plane + t) % PLANES * HEADS + head, (plane + t) % PLANES) for t in range(1, PLANES)]
-    slide_peers = [(slide + t) % PLANES for t in range(1, PLANES)]
-
-    def remote(stage, source, target, axis, peer, mine, theirs):
+
+    def remote(stage, source, target, where, mine, theirs):
         send_copy = pltpu.make_async_remote_copy(
             src_ref=source,
             dst_ref=target,
             send_sem=send_sem.at[stage, theirs],
             recv_sem=recv_sem.at[stage, mine],
-            device_id={axis: peer},
+            device_id=where,
             device_id_type=MESH,
         )
         send_copy.start()
@@ -128,7 +155,7 @@
             dst_ref=target,
             send_sem=send_sem.at[stage, theirs],
             recv_sem=recv_sem.at[stage, theirs],
-            device_id={axis: peer},
+            device_id=where,
             device_id_type=MESH,
         )
         return wait_copy
@@ -155,18 +182,13 @@
 
     def launch(stage, first, last):
         copies = [
-            remote(stage, send.at[to, first:last], all_t.at[first:last, my_lanes], "seq", peer, head, to)
+            remote(stage, send.at[to, first:last], all_t.at[first:last, my_lanes], {"seq": peer}, head, to)
             for peer, to in plane_peers
         ]
         return copies + [own_copy(stage, send.at[head, first:last], all_t.at[first:last, my_lanes])]
 
     stage_in(1, key_ref[...].T)
     stage_in(0, query_ref[...].T)
-    barrier = pltpu.get_barrier_semaphore()
-    for peer, _ in plane_peers + far_peers:
-        pl.semaphore_signal(barrier, inc=1, device_id={"seq": peer}, device_id_type=MESH)
-    for peer in slide_peers:
-        pl.semaphore_signal(barrier, inc=1, device_id={"slide": peer}, device_id_type=MESH)
     pl.semaphore_wait(barrier, 13)
     first = launch(0, 0, 96)
     stage_in(2, value_ref[...].T)
@@ -230,31 +252,65 @@
     near_tiles(96, 144)
     far_send[...] = dot(all_t[48:144, 4096:5120], pick).astype(BF)
     fourth = [
-        remote(3, far_send, far_land.at[plane], "seq", peer, plane, to) for peer, to in far_peers
+        remote(3, far_send, far_land.at[plane], {"seq": peer}, plane, to) for peer, to in far_peers
     ] + [own_copy(3, far_send, far_land.at[plane])]
     for g in range(5):
         build_value(g)
 
-    def forward(i):
-        key_from = pl.multiple_of(i // 4 * 1024, 1024)
+    def peak_of(score):
+        return jnp.max(score.reshape(32, 8, BLOCK), axis=0)
+
+    def score_of(i, c):
+        key_from = pl.multiple_of(i // 4 * 1024 + CHUNK * c, CHUNK)
         query_from = pl.multiple_of(i * BLOCK, BLOCK)
-        score = dot(key_a[pl.ds(key_from, 1024), :], query_a[:, pl.ds(query_from, BLOCK)])
-        peak = jnp.max(score, axis=0, keepdims=True)
-        prob = jnp.exp2(score - peak).astype(BF)
-        probs[i] = prob
-        outs[:, pl.ds(query_from, BLOCK)] = dot(value_t[0:64, pl.ds(key_from, 1024)], prob)
+        return dot(key_a[pl.ds(key_from, CHUNK), :], query_a[:, pl.ds(query_from, BLOCK)])
+
+    def weigh(i, held, top, ahead, ahead_top, following):
+        query_from = pl.multiple_of(i * BLOCK, BLOCK)
+        peak = jnp.max(top[...], axis=0, keepdims=True)
+        most = None
+        gathered = jnp.zeros((64, BLOCK), F32)
+        for c in range(1024 // CHUNK):
+            rows = slice(CHUNK * c, CHUNK * c + CHUNK)
+            if following is not None:
+                score = score_of(following, c)
+                ahead[rows, :] = score
+                reach = peak_of(score)
+                most = reach if most is None else jnp.maximum(most, reach)
+            prob = jnp.exp2(held[rows, :] - peak).astype(BF)
+            probs[i, rows, :] = prob
+            key_from = pl.multiple_of(i // 4 * 1024 + CHUNK * c, CHUNK)
+            gathered = gathered + dot(value_t[0:64, pl.ds(key_from, CHUNK)], prob)
+        outs[:, pl.ds(query_from, BLOCK)] = gathered
         stats[:, pl.ds(query_from, BLOCK)] = jnp.broadcast_to(peak, (8, BLOCK))
-
-    @pl.loop(0, BLOCKS - 1)
-    def _(i):
-        forward(i)
-
+        if following is not None:
+            ahead_top[...] = most
+
+    def begin(i, held, top):
+        most = None
+        for c in range(1024 // CHUNK):
+            score = score_of(i, c)
+            held[CHUNK * c : CHUNK * c + CHUNK, :] = score
+            reach = peak_of(score)
+            most = reach if most is None else jnp.maximum(most, reach)
+        top[...] = most
+
+    begin(0, score_a, top_a)
+
+    @pl.loop(0, 9)
+    def _(j):
+        weigh(2 * j, score_a, top_a, score_b, top_b, 2 * j + 1)
+        weigh(2 * j + 1, score_b, top_b, score_a, top_a, 2 * j + 2)
+
+    weigh(18, score_a, top_a, score_b, top_b, 19)
+    weigh(19, score_b, top_b, score_a, top_a, None)
     wait_all(fourth)
     for z in range(PLANES):
         all_t[48:144, 5120 + 256 * z : 5376 + 256 * z] = far_land[z]
     build_key(5)
     build_value(5)
-    forward(BLOCKS - 1)
+    begin(BLOCKS - 1, score_a, top_a)
+    weigh(BLOCKS - 1, score_a, top_a, score_b, top_b, None)
     wait_all(third)
     near_tiles(144, 192)
     all_t[144:192, 5120:5376] = dot(all_t[144:192, 4096:5120], pick).astype(BF)
@@ -319,7 +375,7 @@
         write_grad(5120 + 128 * t, 128, far_dot[t], far_ratio[t])
     grad_a[64:128, :] = jnp.zeros((64, LANES_QUERY), BF)
     fifth = [
-        remote(4, att_send.at[to], land.at[head, 0:48], "seq", peer, head, to) for peer, to in plane_peers
+        remote(4, att_send.at[to], land.at[head, 0:48], {"seq": peer}, head, to) for peer, to in plane_peers
     ] + [own_copy(4, att_send.at[head], land.at[head, 0:48])]
 
     @pl.loop(0, BLOCKS)
@@ -327,11 +383,10 @@
         query_from = pl.multiple_of(i * BLOCK, BLOCK)
         lanes = pl.ds(query_from, BLOCK)
         gap = jnp.zeros((16, BLOCK), BF)
-        wide = jnp.zeros((64, BLOCK), BF)
-        top = jnp.concatenate([all_t[0:48, lanes], gap, wide], axis=0)
-        low = jnp.concatenate([wide, grad_a[0:48, lanes], gap], axis=0)
-        right[i, 0:BLOCK, :] = top.T
-        right[i, BLOCK : 2 * BLOCK, :] = low.T
+        both = jnp.concatenate([all_t[0:48, lanes], gap, grad_a[0:48, lanes], gap], axis=0).T
+        left = lax.broadcasted_iota(jnp.int32, (BLOCK, 128), 1) < 64
+        right[i, 0:BLOCK, :] = jnp.where(left, both, jnp.zeros_like(both))
+        right[i, BLOCK : 2 * BLOCK, :] = jnp.where(left, jnp.zeros_like(both), both)
 
     sums[...] = jnp.zeros((LANES_ALL, 128), F32)
 
@@ -345,8 +400,8 @@
         both = jnp.concatenate([slope, prob], axis=1)
         sums[pl.ds(key_from, 1024), :] += dot(both, right[i])
 
-    def backward_part(g):
-        @pl.loop(0, 4)
+    def backward_part(g, first, count=2):
+        @pl.loop(first, first + count)
         def _(i):
             backward(4 * g + i)
 
@@ -356,9 +411,9 @@
         far_part[z, 0:48, :] = far_t[0:48, 256 * z : 256 * z + 256].astype(BF)
         far_part[z, 48:96, :] = far_t[64:112, 256 * z : 256 * z + 256].astype(BF)
     sixth = [
-        remote(5, far_part.at[to], far_back.at[plane], "seq", peer, plane, to) for peer, to in far_peers
+        remote(5, far_part.at[to], far_back.at[plane], {"seq": peer}, plane, to) for peer, to in far_peers
     ] + [own_copy(5, far_part.at[plane], far_back.at[plane])]
-    backward_part(4)
+    backward_part(4, 0, 4)
 
     def collect(part, half):
         pieces = []
@@ -375,10 +430,10 @@
         att = dot_nt(collect(0, half), orders[half][...]).astype(BF)
         part = dot(att, grad_ref[...]).astype(BF)
         for turn in range(4):
-            first_send[4 * half + turn] = part[48 * turn : 48 * turn + 48]
-    seventh = [
-        remote(6, first_send.at[to], first_land.at[head], "seq", peer, head, to) for peer, to in plane_peers
-    ] + [own_copy(6, first_send.at[head], first_land.at[head])]
+            core_send[half, turn] = part[48 * turn : 48 * turn + 48]
+    core_copies = [
+        remote(6, core_send.at[1 - core], core_land, {"slide": other_core}, core, 1 - core)
+    ]
 
     wait_all(sixth)
     far_sum = far_back[0].astype(F32)
@@ -395,10 +450,53 @@
             value = value + ref[t].astype(F32)
         return value
 
+    flying = {0: core_copies}
+
+    def advance(point):
+        if point not in POINTS:
+            return
+        stage = POINTS.index(point)
+        wait_all(flying[stage])
+        if stage == 0:
+            for z in range(PLANES):
+                far_first[z] = (
+                    core_send[core, z].astype(F32) + core_land[z].astype(F32)
+                ).astype(BF)
+            flying[1] = [
+                remote(7, far_first.at[to], far_second.at[plane], {"seq": peer}, plane, to)
+                for peer, to in far_peers
+            ] + [own_copy(7, far_first.at[plane], far_second.at[plane])]
+        if stage == 1:
+            ring_part[...] = total(far_second).astype(BF)
+            flying[2] = [
+                remote(8, ring_part, ring_land.at[flat], {"seq": peer}, flat, to)
+                for peer, to in ring_peers
+            ] + [own_copy(8, ring_part, ring_land.at[flat])]
+        if stage == 2:
+            cross_part[...] = total(ring_land).astype(BF)
+            mine = across * 2 + tall
+            flying[3] = [
+                remote(9, cross_part, cross_land.at[mine], where, mine, to)
+                for where, to in cross_peers
+            ] + [own_copy(9, cross_part, cross_land.at[mine])]
+        if stage == 3:
+            last_part[...] = (total(cross_land) * (65536.0**-0.5)).astype(BF)
+            flying[4] = [
+                remote(10, last_part, last_land.at[plane], {"seq": peer}, plane, to)
+                for peer, to in far_peers
+            ] + [own_copy(10, last_part, last_land.at[plane])]
+        if stage == 4:
+            flying[5] = [
+                remote(11, last_land, final_land, {"slide": other_core}, core, 1 - core)
+            ]
+
     returned = []
     for turn in range(1, 5):
         g = (head // 2 + turn) % 4
-        backward_part(g)
+        backward_part(g, 0)
+        advance(2 * turn - 1)
+        backward_part(g, 2)
+        advance(2 * turn)
         for e in range(2):
             s = 2 * g + e
             lanes = pl.ds(pl.multiple_of(128 * s, 128), 128)
@@ -417,37 +515,21 @@
             give[s, 96:144, 128:512] = own_t[64:112, 128:512].astype(BF)
             target = land.at[head, 48:192]
             if turn < 4:
-                returned.append(remote(7, give.at[s], target, "seq", plane * HEADS + s, head, s))
+                returned.append(remote(12, give.at[s], target, {"seq": plane * HEADS + s}, head, s))
         if turn == 4:
             other = head + 1 - 2 * (head % 2)
             returned.append(
-                remote(7, give.at[other], target, "seq", plane * HEADS + other, head, other)
+                remote(12, give.at[other], target, {"seq": plane * HEADS + other}, head, other)
             )
-            returned.append(own_copy(7, give.at[head], target))
-        if turn == 1:
-            wait_all(seventh)
-            plane_part[...] = total(first_land).astype(BF)
-            eighth = [
-                remote(8, plane_part, plane_land.at[plane], "seq", peer, plane, to)
-                for peer, to in far_peers
-            ] + [own_copy(8, plane_part, plane_land.at[plane])]
-        if turn == 2:
-            wait_all(eighth)
-            slide_part[...] = total(plane_land).astype(BF)
-            ninth = [
-                remote(9, slide_part, slide_land.at[slide], "slide", peer, slide, peer)
-                for peer in slide_peers
-            ] + [own_copy(9, slide_part, slide_land.at[slide])]
-        if turn == 3:
-            wait_all(ninth)
-            last_part[...] = (total(slide_land) * (65536.0**-0.5)).astype(BF)
-            tenth = [
-                remote(10, last_part, last_land.at[head], "seq", peer, head, to)
-                for peer, to in plane_peers
-            ] + [own_copy(10, last_part, last_land.at[head])]
-    wait_all(tenth)
-    for h in range(HEADS):
-        weight_out[48 * h : 48 * h + 48, :] = last_land[h].astype(F32)
+            returned.append(own_copy(12, give.at[head], target))
+    advance(9)
+    for z in range(PLANES):
+        spot = pl.multiple_of(core * 192 + 48 * z, 48)
+        weight_out[pl.ds(spot, 48), :] = last_land[z].astype(F32)
+    wait_all(flying[5])
+    for z in range(PLANES):
+        spot = pl.multiple_of((1 - core) * 192 + 48 * z, 48)
+        weight_out[pl.ds(spot, 48), :] = final_land[z].astype(F32)
     wait_all(returned)
     for part, target in ((1, query_out), (2, key_out), (3, value_out)):
         for half in range(2):
@@ -494,19 +576,26 @@
             pltpu.VMEM((144, 1024), F32),
             pltpu.VMEM((HEADS, 144, ROWS), BF),
             pltpu.VMEM((HEADS, 192, ROWS), BF),
-            pltpu.VMEM((HEADS, 48, DEPTH), BF),
-            pltpu.VMEM((HEADS, 48, DEPTH), BF),
+            pltpu.VMEM((2, PLANES, 48, DEPTH), BF),
+            pltpu.VMEM((PLANES, 48, DEPTH), BF),
+            pltpu.VMEM((PLANES, 48, DEPTH), BF),
+            pltpu.VMEM((PLANES, 48, DEPTH), BF),
             pltpu.VMEM((48, DEPTH), BF),
             pltpu.VMEM((PLANES, 48, DEPTH), BF),
             pltpu.VMEM((48, DEPTH), BF),
             pltpu.VMEM((PLANES, 48, DEPTH), BF),
             pltpu.VMEM((48, DEPTH), BF),
-            pltpu.VMEM((HEADS, 48, DEPTH), BF),
+            pltpu.VMEM((PLANES, 48, DEPTH), BF),
+            pltpu.VMEM((PLANES, 48, DEPTH), BF),
+            pltpu.VMEM((1024, BLOCK), F32),
+            pltpu.VMEM((1024, BLOCK), F32),
+            pltpu.VMEM((8, BLOCK), F32),
+            pltpu.VMEM((8, BLOCK), F32),
             pltpu.VMEM((ROWS, ROWS), BF),
             pltpu.VMEM((ROWS, ROWS), BF),
-            sems((11, HEADS)),
-            sems((11, HEADS)),
-            sems((11,)),
+            sems((13, HEADS)),
+            sems((13, HEADS)),
+            sems((13,)),
         ],
         compiler_params=pltpu.CompilerParams(
             collective_id=0, has_side_effects=True, vmem_limit_bytes=VMEM_LIMIT

time: 99 us -> 83.9 us (0.85)
  Pallas kernels: 90.6 us -> 75.8 us
    pallas_call x1, Pallas kernels: 90.6 us -> 75.8 us  [local(): pl.pallas_call(fused_kernel, out_shape=(jax.ShapeDtypeStruct((ROWS, WIDTH...]
where the time goes in v3:
time: 83.9 us; the launch traced here: 82.5 us
  Pallas kernels  75.8 us (90%)
  local copies, waits for them, and re-layouts  5.44 us (6%)
  between operations  1.3 us (2%)
    pallas_call x1, Pallas kernels, local(): pl.pallas_call(fused_kernel, out_shape=(jax.ShapeDtypeStruct((ROWS, WIDTH...  75.8 us
    unnamed x8, local copies, waits for them, and re-layouts  5.44 us

profile of v3, /device:TPU:1, one launch (start us, length us, event | category | flops | bytes accessed | tf_op | source)
XLA Modules:
  0.0 82.5 jit_solution(8750101110062032730)
XLA Ops:
  1.3 75.8 %layer_back.1 = (bf16[512,384]{1,0:T(8,128)(2,1)}, bf16[512,384]{1,0:T(8,128)(2,1)}, bf16[512,384]{1,0:T(8,128)(2,1)}, f32[384,768]{1,0:T(8,128)}) custom-call(s32[1]{0:T(128)S(6)} %copy.14.count_ref, bf16[512,384]{1,0:T(8,128)(2,1)} %query_ref.1, bf16[512,384]{1,0:T(8,128)(2,1)} %key_ref.1, bf16[512,384]{1,0:T(8,128)(2,1)} %value_ref.1, ...), custom_call_target="tpu_custom_call" | custom-call | tf_op jit(solution)/shard_map/layer_back/pallas_call | solution.py:548
  77.1 0.0 copy-start.1
  77.1 0.0 copy-start
  77.1 1.9 %copy.15 = bf16[512,384]{1,0:T(8,128)(2,1)} copy(bf16[512,384]{1,0:T(8,128)(2,1)} %get-tuple-element.8) | data formatting | bytes 786432
  79.0 1.8 %copy.16 = bf16[512,384]{1,0:T(8,128)(2,1)} copy(bf16[512,384]{1,0:T(8,128)(2,1)} %get-tuple-element.9) | data formatting | bytes 786432
  80.8 0.0 copy-done.1
  80.8 0.7 copy.17
  81.5 0.0 copy-done
  81.5 1.0 %copy.18 = f32[384,768]{1,0:T(8,128)} copy(f32[384,768]{1,0:T(8,128)S(1)} %copy-done) | data formatting | bytes 2359296
Async XLA Ops:
  77.1 3.7 %copy-start.1 = (bf16[512,384]{1,0:T(8,128)(2,1)S(1)}, bf16[512,384]{1,0:T(8,128)(2,1)}, u32[]{:S(2)}) copy-start(bf16[512,384]{1,0:T(8,128)(2,1)} %get-tuple-element.10) | copy-start | bytes 1179652
  77.1 4.4 %copy-start = (f32[384,768]{1,0:T(8,128)S(1)}, f32[384,768]{1,0:T(8,128)}, u32[]{:S(2)}) copy-start(f32[384,768]{1,0:T(8,128)} %get-tuple-element.11) | copy-start | bytes 3538948

commit v4 on v3

--- a/solution.py
+++ b/solution.py
@@ -17,6 +17,7 @@
 BLOCK = 256
 BLOCKS = LANES_QUERY // BLOCK
 CHUNK = 256
+CHUNK_BACK = 512
 DEAD = -1e30
 SCALE = float(HEAD_WIDTH) ** -0.5
 SCALE_TWO = SCALE * 1.4426950408889634
@@ -41,7 +42,7 @@
 
 def order_matrix(swap):
     rows = lax.broadcasted_iota(jnp.int32, (ROWS, ROWS), 0)
-    slots = lax.broadcasted_iota(jnp.int32, (ROWS, ROWS), 1)
+    slots = lax.broadcasted_iota(jnp.int32, (1, ROWS), 1)
     return jnp.where(rows == row_of(slots, swap), 1.0, 0.0).astype(BF)
 
 
@@ -57,19 +58,28 @@
 
 
 MESH = pl.DeviceIdType.MESH
-POINTS = (1, 3, 5, 7, 9)
+POINTS = (0, 2, 5, 9)
+
+
+def collect(land, part, half):
+    pieces = []
+    for turn in range(4):
+        rows = land[4 * half + turn, 48 * part : 48 * part + 48, :]
+        if turn:
+            cut = 512 - 128 * turn
+            rows = jnp.concatenate([rows[:, cut:], rows[:, :cut]], axis=1)
+        pieces.append(rows)
+    return jnp.concatenate(pieces, axis=0)
 
 
 def fused_kernel(
     count_ref,
-    query_ref,
-    key_ref,
-    value_ref,
-    grad_ref,
-    weight_ref,
-    query_out,
-    key_out,
-    value_out,
+    query_hbm,
+    key_hbm,
+    value_hbm,
+    grad_hbm,
+    weight_hbm,
+    land,
     weight_out,
     send,
     all_t,
@@ -90,53 +100,68 @@
     far_back,
     far_wide,
     give,
-    land,
+    att_land,
     core_send,
     core_land,
-    far_first,
-    far_second,
-    ring_part,
-    ring_land,
-    cross_part,
-    cross_land,
+    group_part,
+    group_land,
+    plane_part,
+    plane_land,
     last_part,
-    last_land,
-    final_land,
     score_a,
     score_b,
     top_a,
     top_b,
     order_a,
     order_b,
+    query_ref,
+    key_ref,
+    value_ref,
+    grad_ref,
+    weight_ref,
     send_sem,
     recv_sem,
     own_sem,
+    load_sem,
 ):
     plane, head = place()
     slide = lax.axis_index("slide")
     count = count_ref[0]
     core = slide % 2
     across = slide // 2
-    tall, flat = head // 4, head % 4
     barrier = pltpu.get_barrier_semaphore()
     orders = (order_a, order_b)
     plane_peers = [(plane * HEADS + (head + t) % HEADS, (head + t) % HEADS) for t in range(1, HEADS)]
     far_peers = [((plane + t) % PLANES * HEADS + head, (plane + t) % PLANES) for t in range(1, PLANES)]
-    ring_peers = [
-        (plane * HEADS + tall * 4 + (flat + t) % 4, (flat + t) % 4) for t in range(1, PLANES)
-    ]
     other_core = slide + 1 - 2 * core
-    cross_peers = []
-    for step_across, step_tall in ((0, 1), (1, 0), (1, 1)):
-        to_across = across + step_across * (1 - 2 * across)
-        to_tall = tall + step_tall * (1 - 2 * tall)
-        where = {"slide": to_across * 2 + core, "seq": plane * HEADS + to_tall * 4 + flat}
-        cross_peers.append((where, to_across * 2 + to_tall))
-    for peer, _ in plane_peers + far_peers:
+    group_peers = []
+    for step_plane in range(PLANES):
+        for step_across in range(2):
+            if step_plane or step_across:
+                to_plane = (plane + step_plane) % PLANES
+                to_across = across + step_across * (1 - 2 * across)
+                where = {"slide": to_across * 2 + core, "seq": to_plane * HEADS + head}
+                group_peers.append((where, to_plane * 2 + to_across))
+    group_place = plane * 2 + across
+    for peer, _ in plane_peers:
         pl.semaphore_signal(barrier, inc=1, device_id={"seq": peer}, device_id_type=MESH)
     pl.semaphore_signal(barrier, inc=1, device_id={"slide": other_core}, device_id_type=MESH)
-    for where, _ in cross_peers[1:]:
+    for where, _ in group_peers:
         pl.semaphore_signal(barrier, inc=1, device_id=where, device_id_type=MESH)
+    loads = [
+        pltpu.make_async_copy(source, target, load_sem.at[n])
+        for n, (source, target) in enumerate(
+            (
+                (key_hbm, key_ref),
+                (value_hbm, value_ref),
+                (query_hbm, query_ref),
+                (grad_hbm, grad_ref),
+                (weight_hbm, weight_ref),
+            )
+        )
+    ]
+    for load in loads:
+        load.start()
     order_a[...] = order_matrix(False)
     order_b[...] = order_matrix(True)
 
@@ -187,12 +212,17 @@
         ]
         return copies + [own_copy(stage, send.at[head, first:last], all_t.at[first:last, my_lanes])]
 
+    loads[0].wait()
     stage_in(1, key_ref[...].T)
+    loads[1].wait()
+    stage_in(2, value_ref[...].T)
+    pl.semaphore_wait(barrier, 15)
+    first = launch(0, 48, 144)
+    loads[2].wait()
     stage_in(0, query_ref[...].T)
-    pl.semaphore_wait(barrier, 13)
-    first = launch(0, 0, 96)
-    stage_in(2, value_ref[...].T)
-    second = launch(1, 96, 144)
+    second = launch(1, 0, 48)
+    loads[3].wait()
+    loads[4].wait()
     lane = lax.broadcasted_iota(jnp.int32, (1, ROWS), 1)
     own_live = (plane * SPAN + head * ROWS + lane < count).astype(F32)
     back = (dot_nt(weight_ref[...], grad_ref[...]) * own_live).astype(BF)
@@ -219,7 +249,7 @@
     value_t[48:64, :] = jnp.ones((16, LANES_ALL), BF)
     value_t[64:128, :] = jnp.zeros((64, LANES_ALL), BF)
     here = lax.broadcasted_iota(jnp.int32, (1024, 256), 0)
-    there = lax.broadcasted_iota(jnp.int32, (1024, 256), 1)
+    there = lax.broadcasted_iota(jnp.int32, (1, 256), 1)
     pick = jnp.where(here == there // 32 * 128 + there % 32, 1.0, 0.0).astype(BF)
 
     def near_tiles(first, last):
@@ -243,19 +273,18 @@
         value_a[lanes, :] = value_t[:, lanes].T
 
     wait_all(first)
-    near_tiles(0, 96)
-    all_t[0:48, 5120:5376] = dot(all_t[0:48, 4096:5120], pick).astype(BF)
-    build_query(0, LANES_QUERY)
-    for g in range(5):
-        build_key(g)
-    wait_all(second)
-    near_tiles(96, 144)
+    near_tiles(48, 144)
     far_send[...] = dot(all_t[48:144, 4096:5120], pick).astype(BF)
     fourth = [
         remote(3, far_send, far_land.at[plane], {"seq": peer}, plane, to) for peer, to in far_peers
     ] + [own_copy(3, far_send, far_land.at[plane])]
     for g in range(5):
+        build_key(g)
         build_value(g)
+    wait_all(second)
+    near_tiles(0, 48)
+    all_t[0:48, 5120:5376] = dot(all_t[0:48, 4096:5120], pick).astype(BF)
+    build_query(0, LANES_QUERY)
 
     def peak_of(score):
         return jnp.max(score.reshape(32, 8, BLOCK), axis=0)
@@ -339,6 +368,7 @@
         dots = jnp.sum(att.astype(F32) * back, axis=0, keepdims=True)
         return att, dots, inverse
 
+    later = []
     for s in range(HEADS):
         first = 512 * s
         near_from = 4096 + 128 * s
@@ -356,8 +386,8 @@
         total = out_a * gain_a + out_b * gain_b + out_c * gain_c
         att, dots, inverse = finish(first, 128, total, live_row[:, first : first + 128])
         att_send[s, :, 0:128] = att
-        write_grad(first, 128, dots, gain_a * inverse)
-        write_grad(near_from, 128, dots, gain_b * inverse)
+        later.append((first, 128, dots, gain_a * inverse))
+        later.append((near_from, 128, dots, gain_b * inverse))
         shift = 32 * (s % 4)
         packed_ratio = jnp.broadcast_to(jnp.where(inside, gain_c * inverse, 0.0), (8, 128))
         packed_dot = jnp.broadcast_to(jnp.where(inside, dots, 0.0), (8, 128))
@@ -370,13 +400,15 @@
             first + 128, 384, outs[:, first + 128 : first + 512], live_row[:, first + 128 : first + 512]
         )
         att_send[s, :, 128:512] = att
-        write_grad(first + 128, 384, dots, inverse)
+        later.append((first + 128, 384, dots, inverse))
+    fifth = [
+        remote(4, att_send.at[to], att_land.at[head], {"seq": peer}, head, to) for peer, to in plane_peers
+    ] + [own_copy(4, att_send.at[head], att_land.at[head])]
+    for item in later:
+        write_grad(*item)
     for t in range(2):
         write_grad(5120 + 128 * t, 128, far_dot[t], far_ratio[t])
     grad_a[64:128, :] = jnp.zeros((64, LANES_QUERY), BF)
-    fifth = [
-        remote(4, att_send.at[to], land.at[head, 0:48], {"seq": peer}, head, to) for peer, to in plane_peers
-    ] + [own_copy(4, att_send.at[head], land.at[head, 0:48])]
 
     @pl.loop(0, BLOCKS)
     def _(i):
@@ -390,22 +422,32 @@
 
     sums[...] = jnp.zeros((LANES_ALL, 128), F32)
 
-    def backward(i):
-        key_from = pl.multiple_of(i // 4 * 1024, 1024)
+    def change_of(i, c):
+        key_from = pl.multiple_of(i // 4 * 1024 + CHUNK_BACK * c, CHUNK_BACK)
         query_from = pl.multiple_of(i * BLOCK, BLOCK)
-        change = dot(value_a[pl.ds(key_from, 1024), :], grad_a[:, pl.ds(query_from, BLOCK)])
-        prob = probs[i]
-        slope = (prob.astype(F32) * change).astype(BF)
-        outs[0:48, pl.ds(query_from, BLOCK)] = dot(all_t[48:96, pl.ds(key_from, 1024)], slope)
-        both = jnp.concatenate([slope, prob], axis=1)
-        sums[pl.ds(key_from, 1024), :] += dot(both, right[i])
-
-    def backward_part(g, first, count=2):
-        @pl.loop(first, first + count)
-        def _(i):
-            backward(4 * g + i)
-
-    backward(BLOCKS - 1)
+        return dot(value_a[pl.ds(key_from, CHUNK_BACK), :], grad_a[:, pl.ds(query_from, BLOCK)])
+
+    def backward(i, held, ahead, following):
+        query_from = pl.multiple_of(i * BLOCK, BLOCK)
+        gathered = jnp.zeros((48, BLOCK), F32)
+        for c in range(1024 // CHUNK_BACK):
+            rows = slice(CHUNK_BACK * c, CHUNK_BACK * c + CHUNK_BACK)
+            if following is not None:
+                ahead[rows, :] = change_of(following, c)
+            prob = probs[i, rows, :]
+            slope = (prob.astype(F32) * held[rows, :]).astype(BF)
+            keys = pl.ds(pl.multiple_of(i // 4 * 1024 + CHUNK_BACK * c, CHUNK_BACK), CHUNK_BACK)
+            sums[keys, :] += dot(jnp.concatenate([slope, prob], axis=1), right[i])
+            gathered = gathered + dot(all_t[48:96, keys], slope)
+        outs[0:48, pl.ds(query_from, BLOCK)] = gathered
+
+    def backward_pair(i, following):
+        backward(i, score_a, score_b, i + 1)
+        backward(i + 1, score_b, score_a, following)
+
+    for c in range(1024 // CHUNK_BACK):
+        score_b[CHUNK_BACK * c : CHUNK_BACK * c + CHUNK_BACK, :] = change_of(BLOCKS - 1, c)
+    backward(BLOCKS - 1, score_b, score_a, 16)
     far_t = sums[5120:6144, :].T
     for z in range(PLANES):
         far_part[z, 0:48, :] = far_t[0:48, 256 * z : 256 * z + 256].astype(BF)
@@ -413,24 +455,16 @@
     sixth = [
         remote(5, far_part.at[to], far_back.at[plane], {"seq": peer}, plane, to) for peer, to in far_peers
     ] + [own_copy(5, far_part.at[plane], far_back.at[plane])]
-    backward_part(4, 0, 4)
-
-    def collect(part, half):
-        pieces = []
-        for turn in range(4):
-            rows = land[4 * half + turn, 48 * part : 48 * part + 48, :]
-            if turn:
-                cut = 512 - 128 * turn
-                rows = jnp.concatenate([rows[:, cut:], rows[:, :cut]], axis=1)
-            pieces.append(rows)
-        return jnp.concatenate(pieces, axis=0)
+    backward_pair(16, 18)
+    backward_pair(18, 4 * ((head // 2 + 1) % 4))
 
     wait_all(fifth)
     for half in range(2):
-        att = dot_nt(collect(0, half), orders[half][...]).astype(BF)
+        att = dot_nt(collect(att_land, 0, half), orders[half][...]).astype(BF)
         part = dot(att, grad_ref[...]).astype(BF)
         for turn in range(4):
-            core_send[half, turn] = part[48 * turn : 48 * turn + 48]
+            for wing in range(2):
+                core_send[half, turn, wing] = part[48 * turn : 48 * turn + 48, 384 * wing : 384 * wing + 384]
     core_copies = [
         remote(6, core_send.at[1 - core], core_land, {"slide": other_core}, core, 1 - core)
     ]
@@ -459,44 +493,38 @@
         wait_all(flying[stage])
         if stage == 0:
             for z in range(PLANES):
-                far_first[z] = (
-                    core_send[core, z].astype(F32) + core_land[z].astype(F32)
-                ).astype(BF)
+                for wing in range(2):
+                    group_part[2 * z + wing] = (
+                        core_send[core, z, wing].astype(F32) + core_land[z, wing].astype(F32)
+                    ).astype(BF)
             flying[1] = [
-                remote(7, far_first.at[to], far_second.at[plane], {"seq": peer}, plane, to)
-                for peer, to in far_peers
-            ] + [own_copy(7, far_first.at[plane], far_second.at[plane])]
+                remote(7, group_part.at[to], group_land.at[group_place], where, group_place, to)
+                for where, to in group_peers
+            ] + [own_copy(7, group_part.at[group_place], group_land.at[group_place])]
         if stage == 1:
-            ring_part[...] = total(far_second).astype(BF)
+            plane_part[...] = total(group_land).astype(BF)
             flying[2] = [
-                remote(8, ring_part, ring_land.at[flat], {"seq": peer}, flat, to)
-                for peer, to in ring_peers
-            ] + [own_copy(8, ring_part, ring_land.at[flat])]
+                remote(8, plane_part, plane_land.at[head], {"seq": peer}, head, to)
+                for peer, to in plane_peers
+            ] + [own_copy(8, plane_part, plane_land.at[head])]
         if stage == 2:
-            cross_part[...] = total(ring_land).astype(BF)
-            mine = across * 2 + tall
+            last_part[...] = (total(plane_land) * (65536.0**-0.5)).astype(BF)
             flying[3] = [
-                remote(9, cross_part, cross_land.at[mine], where, mine, to)
-                for where, to in cross_peers
-            ] + [own_copy(9, cross_part, cross_land.at[mine])]
+                remote(9, last_part, weight_out.at[core, group_place], where, group_place, to)
+                for where, to in group_peers
+            ] + [own_copy(9, last_part, weight_out.at[core, group_place])]
         if stage == 3:
-            last_part[...] = (total(cross_land) * (65536.0**-0.5)).astype(BF)
             flying[4] = [
-                remote(10, last_part, last_land.at[plane], {"seq": peer}, plane, to)
-                for peer, to in far_peers
-            ] + [own_copy(10, last_part, last_land.at[plane])]
-        if stage == 4:
-            flying[5] = [
-                remote(11, last_land, final_land, {"slide": other_core}, core, 1 - core)
+                remote(10, weight_out.at[core], weight_out.at[core], {"slide": other_core}, core, 1 - core)
             ]
 
+    advance(0)
     returned = []
     for turn in range(1, 5):
         g = (head // 2 + turn) % 4
-        backward_part(g, 0)
+        backward_pair(4 * g, 4 * g + 2)
         advance(2 * turn - 1)
-        backward_part(g, 2)
-        advance(2 * turn)
+        backward_pair(4 * g + 2, 4 * ((g + 1) % 4) if turn < 4 else None)
         for e in range(2):
             s = 2 * g + e
             lanes = pl.ds(pl.multiple_of(128 * s, 128), 128)
@@ -513,29 +541,33 @@
             tile = own_t[64:112, 0:128] + near_t[64:112] + far_wide[96:144, lanes]
             give[s, 96:144, 0:128] = tile.astype(BF)
             give[s, 96:144, 128:512] = own_t[64:112, 128:512].astype(BF)
-            target = land.at[head, 48:192]
+            target = land.at[head]
             if turn < 4:
-                returned.append(remote(12, give.at[s], target, {"seq": plane * HEADS + s}, head, s))
+                returned.append(remote(11, give.at[s], target, {"seq": plane * HEADS + s}, head, s))
         if turn == 4:
             other = head + 1 - 2 * (head % 2)
             returned.append(
-                remote(12, give.at[other], target, {"seq": plane * HEADS + other}, head, other)
+                remote(11, give.at[other], target, {"seq": plane * HEADS + other}, head, other)
             )
-            returned.append(own_copy(12, give.at[head], target))
+            returned.append(own_copy(11, give.at[head], target))
+        advance(2 * turn)
     advance(9)
-    for z in range(PLANES):
-        spot = pl.multiple_of(core * 192 + 48 * z, 48)
-        weight_out[pl.ds(spot, 48), :] = last_land[z].astype(F32)
-    wait_all(flying[5])
-    for z in range(PLANES):
-        spot = pl.multiple_of((1 - core) * 192 + 48 * z, 48)
-        weight_out[pl.ds(spot, 48), :] = final_land[z].astype(F32)
+    wait_all(flying[4])
     wait_all(returned)
-    for part, target in ((1, query_out), (2, key_out), (3, value_out)):
+
+
+def unpack_kernel(land_ref, weight_ref, query_out, key_out, value_out, weight_out):
+    orders = (order_matrix(False), order_matrix(True))
+    for part, target in enumerate((query_out, key_out, value_out)):
         for half in range(2):
             target[:, 192 * half : 192 * half + 192] = dot_nt(
-                orders[half][...], collect(part, half)
+                orders[half], collect(land_ref, part, half)
             ).astype(BF)
+    for c in range(2):
+        for z in range(PLANES):
+            for wing in range(2):
+                rows = slice(192 * c + 48 * z, 192 * c + 48 * z + 48)
+                weight_out[rows, 384 * wing : 384 * wing + 384] = weight_ref[c, 2 * z + wing].astype(F32)
 
 
 def vmem(count):
@@ -545,16 +577,14 @@
 def local(tile_count, query_rows, key_rows, value_rows, out_grad, out_weight):
     sems = pltpu.SemaphoreType.DMA
     smem = pl.BlockSpec(memory_space=pltpu.SMEM)
-    return pl.pallas_call(
+    land, weight_part = pl.pallas_call(
         fused_kernel,
         out_shape=(
-            jax.ShapeDtypeStruct((ROWS, WIDTH), BF),
-            jax.ShapeDtypeStruct((ROWS, WIDTH), BF),
-            jax.ShapeDtypeStruct((ROWS, WIDTH), BF),
-            jax.ShapeDtypeStruct((WIDTH, DEPTH), F32),
+            jax.ShapeDtypeStruct((HEADS, 144, ROWS), BF),
+            jax.ShapeDtypeStruct((2, HEADS, 48, WIDTH), BF),
         ),
-        in_specs=[smem] + vmem(5),
-        out_specs=tuple(vmem(4)),
+        in_specs=[smem] + [pl.BlockSpec(memory_space=pl.ANY)] * 5,
+        out_specs=tuple(vmem(2)),
         scratch_shapes=[
             pltpu.VMEM((HEADS, 192, ROWS), BF),
             pltpu.VMEM((192, LANES_ALL), BF),
@@ -575,33 +605,48 @@
             pltpu.VMEM((PLANES, 96, 256), BF),
             pltpu.VMEM((144, 1024), F32),
             pltpu.VMEM((HEADS, 144, ROWS), BF),
-            pltpu.VMEM((HEADS, 192, ROWS), BF),
-            pltpu.VMEM((2, PLANES, 48, DEPTH), BF),
-            pltpu.VMEM((PLANES, 48, DEPTH), BF),
-            pltpu.VMEM((PLANES, 48, DEPTH), BF),
-            pltpu.VMEM((PLANES, 48, DEPTH), BF),
-            pltpu.VMEM((48, DEPTH), BF),
-            pltpu.VMEM((PLANES, 48, DEPTH), BF),
-            pltpu.VMEM((48, DEPTH), BF),
-            pltpu.VMEM((PLANES, 48, DEPTH), BF),
-            pltpu.VMEM((48, DEPTH), BF),
-            pltpu.VMEM((PLANES, 48, DEPTH), BF),
-            pltpu.VMEM((PLANES, 48, DEPTH), BF),
+            pltpu.VMEM((HEADS, 48, ROWS), BF),
+            pltpu.VMEM((2, PLANES, 2, 48, WIDTH), BF),
+            pltpu.VMEM((PLANES, 2, 48, WIDTH), BF),
+            pltpu.VMEM((HEADS, 48, WIDTH), BF),
+            pltpu.VMEM((HEADS, 48, WIDTH), BF),
+            pltpu.VMEM((48, WIDTH), BF),
+            pltpu.VMEM((HEADS, 48, WIDTH), BF),
+            pltpu.VMEM((48, WIDTH), BF),
             pltpu.VMEM((1024, BLOCK), F32),
             pltpu.VMEM((1024, BLOCK), F32),
             pltpu.VMEM((8, BLOCK), F32),
             pltpu.VMEM((8, BLOCK), F32),
             pltpu.VMEM((ROWS, ROWS), BF),
             pltpu.VMEM((ROWS, ROWS), BF),
-            sems((13, HEADS)),
-            sems((13, HEADS)),
-            sems((13,)),
+            pltpu.VMEM((ROWS, WIDTH), BF),
+            pltpu.VMEM((ROWS, WIDTH), BF),
+            pltpu.VMEM((ROWS, WIDTH), BF),
+            pltpu.VMEM((ROWS, DEPTH), BF),
+            pltpu.VMEM((WIDTH, DEPTH), BF),
+            sems((12, HEADS)),
+            sems((12, HEADS)),
+            sems((12,)),
+            sems((5,)),
         ],
         compiler_params=pltpu.CompilerParams(
             collective_id=0, has_side_effects=True, vmem_limit_bytes=VMEM_LIMIT
         ),
         name="layer_back",
     )(tile_count, query_rows, key_rows, value_rows, out_grad, out_weight)
+    return pl.pallas_call(
+        unpack_kernel,
+        out_shape=(
+            jax.ShapeDtypeStruct((ROWS, WIDTH), BF),
+            jax.ShapeDtypeStruct((ROWS, WIDTH), BF),
+            jax.ShapeDtypeStruct((ROWS, WIDTH), BF),
+            jax.ShapeDtypeStruct((WIDTH, DEPTH), F32),
+        ),
+        in_specs=vmem(2),
+        out_specs=tuple(vmem(4)),
+        compiler_params=pltpu.CompilerParams(vmem_limit_bytes=VMEM_LIMIT),
+        name="unpack",
+    )(land, weight_part)
 
 
 def solution(mesh):

time: 83.9 us -> 80.4 us (0.958)
  local copies, waits for them, and re-layouts: 5.44 us -> 0 us
  Pallas kernels: 75.8 us -> 77.6 us
    unnamed x8 -> x0, local copies, waits for them, and re-layouts: 5.44 us -> none
    pallas_call x1 -> x2, Pallas kernels: 75.8 us -> 77.6 us  [the longest x1 73.9 us: local(): pl.pallas_call(fused_kernel, out_shape=(jax.ShapeDtypeStruct((HEADS, 144,...]
where the time goes in v4:
time: 80.4 us; the launch traced here: 78.9 us
  Pallas kernels  77.6 us (97%)
  between operations  1.29 us (2%)
    pallas_call x1, Pallas kernels, local(): pl.pallas_call(fused_kernel, out_shape=(jax.ShapeDtypeStruct((HEADS, 144,...  73.9 us
    pallas_call x1, Pallas kernels, local(): pl.pallas_call(unpack_kernel, out_shape=(jax.ShapeDtypeStruct((ROWS, WIDT...  3.64 us

profile of v4, /device:TPU:1, one launch (start us, length us, event | category | flops | bytes accessed | tf_op | source)
XLA Modules:
  0.0 78.9 jit_solution(15571545792482146042)
XLA Ops:
  1.3 73.9 %layer_back.1 = (bf16[8,144,512]{2,1,0:T(8,128)(2,1)}, bf16[2,8,48,384]{3,2,1,0:T(8,128)(2,1)}) custom-call(s32[1]{0:T(128)S(6)} %copy.10.count_ref, bf16[512,384]{1,0:T(8,128)(2,1)} %query_hbm.1, bf16[512,384]{1,0:T(8,128)(2,1)} %key_hbm.1, bf16[512,384]{1,0:T(8,128)(2,1)} %value_hbm.1, bf16[512,768]{1,0:T(8,128)(2,1)} %grad_hbm.1, bf16[384,768]{1,0:T(8,128)(2,1)} %weight_hbm.1), custom_call_target="tpu_custom_call" | custom-call | tf_op jit(solution)/shard_map/layer_back/pallas_call | solution.py:580
  75.2 3.6 %unpack.1 = (bf16[512,384]{1,0:T(8,128)(2,1)}, bf16[512,384]{1,0:T(8,128)(2,1)}, bf16[512,384]{1,0:T(8,128)(2,1)}, f32[384,768]{1,0:T(8,128)}) custom-call(bf16[8,144,512]{2,1,0:T(8,128)(2,1)} %get-tuple-element.6.land_ref, bf16[2,8,48,384]{3,2,1,0:T(8,128)(2,1)} %get-tuple-element.7.weight_ref), custom_call_target="tpu_custom_call" | custom-call | tf_op jit(solution)/shard_map/unpack/pallas_call | solution.py:637
